TPU v7x, 128 devices: a whole 4x4x4 slice. The times are simulated.
128 devices in a mesh: gz: 4 (over x), xy: 32 (over y, z, core).
Axes of the slice: x: 4, y: 4, z: 4, core: 2. Of those that a mesh axis runs over, the one named last changes fastest.
Arguments:
- em_volume: bfloat16 [32, 8, 128, 128], P('xy', 'gz'), may hold values from -6 to 6
- neighbours: int32 [32, 8], P('xy'), may hold values from -1 to 31, as said below
- first_kernel: bfloat16 [28, 9], replicated, may hold values from -3 to 3
- second_kernel: bfloat16 [28, 28, 27], replicated, may hold values from -0.3125 to 0.3125
- coarse_kernel: bfloat16 [56, 28, 27], replicated, may hold values from -0.3125 to 0.3125
- up_kernel: bfloat16 [28, 56, 4], replicated, may hold values from -1 to 1
- head_kernel: bfloat16 [3, 28], replicated, may hold values from -1.5 to 1.5
Outputs:
- affinity_logits: float32 [32, 3, 8, 128, 128], P('xy', None, 'gz')
Inputs may be any that keep to these rules, and one draw needn't show every extreme that they name: `neighbours`: the blocks occupy distinct positions of one grid of 8 columns; row b lists the blocks at the positions north, south, west, east, north-west, north-east, south-west and south-east of block b, north being the lower row and west the lower column, and -1 where that position holds no block or lies outside the grid. The lists are consistent with the one grid.
All inputs are finite; a program needn't handle non-finite values.
Results may differ from a plain program's by a relative error of at most 0.015.
Values may be sent and summed in bfloat16 or wider, within the bound.
No kernel may reach another device: no remote copies, remote signals or barrier semaphores. Data moves between devices by JAX's collectives and lax.ppermute only.
A program may use at most 256 MiB of HBM per device.

v0:
```python
import jax
import jax.numpy as jnp
from jax import lax
from jax.sharding import PartitionSpec as P


def with_halo(cells, sides, width):
    for axis, dim in sides:
        count = lax.axis_size(axis)
        ends = count - 1
        head = lax.slice_in_dim(cells, 0, width, axis=dim)
        tail = lax.slice_in_dim(cells, cells.shape[dim] - width, cells.shape[dim], axis=dim)
        cells = jnp.concatenate(
            [
                lax.ppermute(tail, axis, [(i, (i + 1) % count) for i in range(ends)]),
                cells,
                lax.ppermute(head, axis, [((i + 1) % count, i) for i in range(ends)]),
            ],
            axis=dim,
        )
    return cells


def exports(features, rim):
    rows = jnp.stack([features[:, :, :, :rim, :], features[:, :, :, -rim:, :]], axis=1)
    sides = jnp.stack([features[:, :, :, :, :rim], features[:, :, :, :, -rim:]], axis=1)
    sides = jnp.swapaxes(sides, -1, -2)
    corners = jnp.stack(
        [
            features[:, :, :, :rim, :rim],
            features[:, :, :, :rim, -rim:],
            features[:, :, :, -rim:, :rim],
            features[:, :, :, -rim:, -rim:],
        ],
        axis=1,
    )
    return (rows, sides, corners)


def zeros_for(parts):
    return tuple((jnp.zeros(item.shape, jnp.float32) for item in parts))


def collector(neighbours):

    def fold(carry, pieces, start):
        rows, sides, corners = pieces
        offsets = jnp.arange(rows.shape[0], dtype=jnp.int32)
        select = (neighbours[:, :, None] == offsets[None, None, :]).astype(rows.dtype)
        new_rows = jnp.einsum(
            "bdj,jdczwx->bdczwx", select[:, 0:2], rows[:, ::-1], preferred_element_type=jnp.float32
        )
        new_sides = jnp.einsum(
            "bdj,jdczwx->bdczwx", select[:, 2:4], sides[:, ::-1], preferred_element_type=jnp.float32
        )
        new_corners = jnp.einsum(
            "bdj,jdczwx->bdczwx",
            select[:, 4:8],
            corners[:, ::-1],
            preferred_element_type=jnp.float32,
        )
        return (new_rows, new_sides, new_corners)

    return fold


def assemble(features, gathered):
    rows, sides, corners = (item.astype(jnp.bfloat16) for item in gathered)
    west = jnp.swapaxes(sides[:, 0], -1, -2)
    east = jnp.swapaxes(sides[:, 1], -1, -2)
    upper = jnp.concatenate([corners[:, 0], rows[:, 0], corners[:, 1]], axis=4)
    middle = jnp.concatenate([west, features, east], axis=4)
    lower = jnp.concatenate([corners[:, 2], rows[:, 1], corners[:, 3]], axis=4)
    return jnp.concatenate([upper, middle, lower], axis=3)


def convolve(extended, kernel, depth):
    planes = extended.shape[2] - depth + 1
    height = extended.shape[3] - 2
    width = extended.shape[4] - 2
    total = None
    for depth_off in range(depth):
        for row_off in range(3):
            for col_off in range(3):
                window = extended[
                    :,
                    :,
                    depth_off : depth_off + planes,
                    row_off : row_off + height,
                    col_off : col_off + width,
                ]
                taps = kernel[:, :, (depth_off * 3 + row_off) * 3 + col_off]
                term = jnp.einsum(
                    "oi,bizyx->bozyx", taps, window, preferred_element_type=jnp.float32
                )
                total = term if total is None else total + term
    return total


def pool(skip):
    blocks, channels, planes, height, width = skip.shape
    grid = skip.astype(jnp.float32).reshape(blocks, channels, planes, height // 2, 2, width // 2, 2)
    return (jnp.sum(grid, axis=(4, 6)) * 0.25).astype(jnp.bfloat16)


def finish(coarse, skip, up_kernel, head_kernel):
    blocks, channels, planes, height, width = coarse.shape
    upward = jnp.einsum("ock,bczyx->bozyxk", up_kernel, coarse, preferred_element_type=jnp.float32)
    upward = upward.reshape(blocks, -1, planes, height, width, 2, 2)
    upward = upward.transpose(0, 1, 2, 3, 5, 4, 6).reshape(
        blocks, -1, planes, 2 * height, 2 * width
    )
    joined = jax.nn.relu(upward + skip.astype(jnp.float32)).astype(jnp.bfloat16)
    return jnp.einsum("kc,bczyx->bkzyx", head_kernel, joined, preferred_element_type=jnp.float32)


def on_device(
    em_volume, neighbours, first_kernel, second_kernel, coarse_kernel, up_kernel, head_kernel
):
    raw = em_volume[:, None]
    fold = collector(neighbours)
    first_taps = first_kernel.reshape(first_kernel.shape[0], 1, 9)
    parts = exports(raw, 1)
    gathered = fold(
        zeros_for(parts),
        (
            lax.all_gather(parts[0], "xy", axis=0, tiled=True),
            lax.all_gather(parts[1], "xy", axis=0, tiled=True),
            lax.all_gather(parts[2], "xy", axis=0, tiled=True),
        ),
        jnp.int32(0),
    )
    inner = jax.nn.relu(convolve(assemble(raw, gathered), first_taps, 1)).astype(jnp.bfloat16)
    parts = exports(inner, 1)
    gathered = fold(
        zeros_for(parts),
        (
            lax.all_gather(parts[0], "xy", axis=0, tiled=True),
            lax.all_gather(parts[1], "xy", axis=0, tiled=True),
            lax.all_gather(parts[2], "xy", axis=0, tiled=True),
        ),
        jnp.int32(0),
    )
    first = assemble(inner, gathered)
    deep_first = with_halo(first, (("gz", 2),), 1)
    skip = jax.nn.relu(convolve(deep_first, second_kernel, 3)).astype(jnp.bfloat16)
    pooled = pool(skip)
    parts = exports(pooled, 1)
    gathered = fold(
        zeros_for(parts),
        (
            lax.all_gather(parts[0], "xy", axis=0, tiled=True),
            lax.all_gather(parts[1], "xy", axis=0, tiled=True),
            lax.all_gather(parts[2], "xy", axis=0, tiled=True),
        ),
        jnp.int32(0),
    )
    wide_pooled = assemble(pooled, gathered)
    deep_pooled = with_halo(wide_pooled, (("gz", 2),), 1)
    coarse = jax.nn.relu(convolve(deep_pooled, coarse_kernel, 3)).astype(jnp.bfloat16)
    return finish(coarse, skip, up_kernel, head_kernel)


def solution(mesh):
    placed = (P("xy", "gz", None, None), P("xy", None), P(), P(), P(), P(), P())
    return jax.shard_map(
        on_device,
        mesh=mesh,
        in_specs=placed,
        out_specs=P("xy", None, "gz", None, None),
        check_vma=False,
    )
```

profile of v0, /device:TPU:1, one launch (start us, length us, event | category | flops | bytes accessed | tf_op | source)
XLA Modules:
  0.0 613.6 jit_solution(12251285022478800161)
XLA Ops:
  2.8 24.2 %all_gather.27 = bf16[32,4,1,2,1,1]{1,3,5,4,2,0:T(2,128)(2,1)S(1)} all-gather(bf16[1,4,1,2,1,1]{1,3,5,4,2,0:T(2,128)(2,1)S(1)} %pad_maximum_fusion.14), channel_id=1, replica_groups=mesh['gz'=4,'xy'=32] {'xy'}, dimensions={0}, use_global_device_ids=true | all-gather | bytes 528 | tf_op jit(solution)/shard_map/all_gather | solution.py:129
  27.8 23.0 %all-gather = bf16[32,2,1,2,128,1]{4,3,5,2,1,0:T(2,128)(2,1)S(1)} all-gather(bf16[1,2,1,2,128,1]{4,3,5,2,1,0:T(2,128)(2,1)S(1)} %pad_maximum_fusion.13), channel_id=2, replica_groups=mesh['gz'=4,'xy'=32] {'xy'}, dimensions={0}, use_global_device_ids=true | all-gather | bytes 33792 | tf_op jit(solution)/shard_map/all_gather | solution.py:128
  51.3 22.4 %all_gather.28 = bf16[32,2,1,2,1,128]{5,3,4,2,1,0:T(2,128)(2,1)S(1)} all-gather(bf16[1,2,1,2,1,128]{5,3,4,2,1,0:T(2,128)(2,1)S(1)} %pad_maximum_fusion.12), channel_id=1, replica_groups=mesh['gz'=4,'xy'=32] {'xy'}, dimensions={0}, use_global_device_ids=true | all-gather | bytes 33792 | tf_op jit(solution)/shard_map/all_gather | solution.py:127
  81.3 23.8 %all_gather.31 = bf16[32,2,28,2,1,128]{5,3,4,2,1,0:T(2,128)(2,1)S(1)} all-gather(bf16[1,2,28,2,1,128]{5,3,4,2,1,0:T(2,128)(2,1)S(1)} %copy.240), channel_id=1, replica_groups=mesh['gz'=4,'xy'=32] {'xy'}, dimensions={0}, use_global_device_ids=true | all-gather | bytes 946176 | tf_op jit(solution)/shard_map/all_gather | solution.py:138
  106.0 22.4 %all_gather.30 = bf16[32,4,28,2,1,1]{2,1,5,4,3,0:T(4,128)(2,1)S(1)} all-gather(bf16[1,4,28,2,1,1]{2,1,5,4,3,0:T(4,128)(2,1)S(1)} %copy.238), channel_id=1, replica_groups=mesh['gz'=4,'xy'=32] {'xy'}, dimensions={0}, use_global_device_ids=true | all-gather | bytes 14784 | tf_op jit(solution)/shard_map/all_gather | solution.py:140
  129.0 3.3 copy.243
  132.3 3.3 copy.244
  135.7 24.0 %all-gather.1 = bf16[32,2,28,2,128,1]{4,3,5,2,1,0:T(2,128)(2,1)S(1)} all-gather(bf16[1,2,28,2,128,1]{4,3,5,2,1,0:T(2,128)(2,1)S(1)} %maximum_bitcast_fusion.1), channel_id=3, replica_groups=mesh['gz'=4,'xy'=32] {'xy'}, dimensions={0}, use_global_device_ids=true | all-gather | bytes 946176 | tf_op jit(solution)/shard_map/all_gather | solution.py:139
  166.1 9.0 %maximum_maximum_fusion.1 = bf16[1,28,2,130,130]{4,1,3,2,0:T(8,128)(2,1)S(1)} fusion(bf16[1,28,2,1,1]{4,1,3,2,0:T(8,128)(2,1)S(1)} %copy.249, bf16[1,28,2,1,128]{4,1,3,2,0:T(8,128)(2,1)S(1)} %get-tuple-element.54, bf16[1,28,2,1,1]{4,1,3,2,0:T(8,128)(2,1)S(1)} %copy.248, bf16[1,28,2,128,1]{4,1,3,2,0:T(8,128)(2,1)} %copy.247, ...), kind=kLoop, calls=%fused_computation.2 | loop fusion | flops 13249600 | bytes 3785600 | tf_op jit(solution)/shard_map/concatenate | solution.py:74
  176.6 3.4 collective-permute-start
  183.0 10.1 %maximum_maximum_fusion.2 = (bf16[1,28,2,129,130]{4,1,3,2,0:T(8,128)(2,1)S(1)}, bf16[1,28,2,129,130]{4,1,3,2,0:T(8,128)(2,1)S(1)}) fusion(bf16[1,28,2,128,1]{4,1,3,2,0:T(8,128)(2,1)S(1)} %copy-done.3, bf16[1,28,2,128,128]{4,1,3,2,0:T(8,128)(2,1)S(1)} %fusion.242, bf16[1,28,2,128,1]{4,1,3,2,0:T(8,128)(2,1)S(1)} %copy-done.2, ...), kind=kLoop, calls=%fused_computation.3 | loop fusion | flops 18782400 | bytes 5649280 | tf_op jit(solution)/shard_map/concatenate | solution.py:74
  210.0 3.6 fusion.19
  213.6 3.1 fusion.23
  216.8 4.7 fusion.38
  222.1 4.6 collective-permute-done.1
  227.2 19.9 %maximum_maximum_fusion = (bf16[1,28,3,130,130]{4,1,3,2,0:T(8,128)(2,1)S(1)}, bf16[1,28,3,130,130]{4,1,3,2,0:T(8,128)(2,1)S(1)}) fusion(bf16[1,28,2,1,1]{4,1,3,2,0:T(8,128)(2,1)S(1)} %copy.249, bf16[1,28,2,1,128]{4,1,3,2,0:T(8,128)(2,1)S(1)} %get-tuple-element.54, bf16[1,28,2,1,1]{4,1,3,2,0:T(8,128)(2,1)S(1)} %copy.248, ...), kind=kLoop, calls=%fused_computation | loop fusion | flops 45427200 | bytes 9464000 | tf_op jit(solution)/shard_map/concatenate | solution.py:13
  247.1 3.3 fusion.10
  287.3 3.2 fusion.7
  296.0 37.5 %fusion.41 = f32[1,28,2,128,128]{4,1,3,2,0:T(8,128)} fusion(bf16[1,28,3,130,130]{4,1,3,2,0:T(8,128)(2,1)} %copy-done.1, f32[2,128,128,28]{2,3,1,0:T(8,128)} %fusion.7, f32[2,128,128,28]{2,3,1,0:T(8,128)} %fusion.8, f32[2,128,128,28]{2,3,1,0:T(8,128)} %fusion.9, f32[2,128,128,28]{2,3,1,0:T(8,128)} %fusion.10, f32[2,128,128,28]{2,3,1,0:T(8,128)} %fusion.11, ...), kind=kOutput, calls=%fused_computation.94 | convolution fusion | flops 77987840 | bytes 114827264 | tf_op jit(solution)/shard_map/oi,bizyx->bozyx/dot_general | solution.py:93
  333.5 10.4 %copy.258 = f32[1,28,2,128,128]{1,4,3,2,0:T(8,128)} copy(f32[1,28,2,128,128]{4,1,3,2,0:T(8,128)} %fusion.41) | data formatting | bytes 7340032 | tf_op jit(solution)/shard_map/convert_element_type | solution.py:102
  343.9 17.7 %reduce_sum.9 = f32[28,2,64,64]{0,3,2,1:T(8,128)} reduce(f32[28,2,64,2,64,2]{0,5,4,3,2,1:T(2,128)} %bitcast.1074, f32[]{:T(128)} %constant.8.clone.1), dimensions={3,5}, to_apply=%region_0.1 | reduce | flops 688128 | bytes 4587524 | tf_op jit(solution)/shard_map/reduce_sum | solution.py:103
  372.2 24.7 %all-gather.2 = bf16[32,2,28,2,64,1]{4,3,5,2,1,0:T(2,128)(2,1)S(1)} all-gather(bf16[1,2,28,2,64,1]{4,3,5,2,1,0:T(2,128)(2,1)S(1)} %maximum_bitcast_fusion.2), channel_id=4, replica_groups=mesh['gz'=4,'xy'=32] {'xy'}, dimensions={0}, use_global_device_ids=true | all-gather | bytes 473088 | tf_op jit(solution)/shard_map/all_gather | solution.py:153
  403.0 23.8 %all_gather.34 = bf16[32,2,28,2,1,64]{5,3,4,2,1,0:T(2,128)(2,1)S(1)} all-gather(bf16[1,2,28,2,1,64]{5,3,4,2,1,0:T(2,128)(2,1)S(1)} %copy.262), channel_id=1, replica_groups=mesh['gz'=4,'xy'=32] {'xy'}, dimensions={0}, use_global_device_ids=true | all-gather | bytes 473088 | tf_op jit(solution)/shard_map/all_gather | solution.py:152
  427.8 22.6 %all_gather.33 = bf16[32,4,28,2,1,1]{2,1,5,4,3,0:T(4,128)(2,1)S(1)} all-gather(bf16[1,4,28,2,1,1]{2,1,5,4,3,0:T(4,128)(2,1)S(1)} %copy.260), channel_id=1, replica_groups=mesh['gz'=4,'xy'=32] {'xy'}, dimensions={0}, use_global_device_ids=true | all-gather | bytes 14784 | tf_op jit(solution)/shard_map/all_gather | solution.py:154
  451.1 4.0 fusion.64
  484.2 6.7 %collective-permute-done.2 = bf16[1,28,1,66,66]{4,3,2,1,0:T(8,128)(2,1)S(1)} collective-permute-done((bf16[1,28,1,66,66]{4,3,2,1,0:T(8,128)(2,1)S(1)}, bf16[1,28,1,66,66]{4,3,2,1,0:T(8,128)(2,1)S(1)}, u32[]{:S(2)}, u32[]{:S(2)}) %collective-permute-start.2) | collective-permute-done | bytes 243968 | tf_op jit(solution)/shard_map/ppermute | solution.py:15
  491.0 3.9 collective-permute-done.3
  495.0 3.9 maximum_maximum_fusion.4
  542.1 34.1 %fusion.42 = f32[2,64,64,28,4]{2,3,4,1,0:T(8,128)} fusion(f32[2,64,64,56]{2,3,1,0:T(8,128)} %fusion.48, f32[2,64,64,56]{2,3,1,0:T(8,128)} %fusion.49, f32[2,64,64,56]{2,3,1,0:T(8,128)} %fusion.50, f32[2,64,64,56]{2,3,1,0:T(8,128)} %fusion.51, f32[2,64,64,56]{2,3,1,0:T(8,128)} %fusion.52, f32[2,64,64,56]{2,3,1,0:T(8,128)} %fusion.53, ...), kind=kOutput, calls=%fused_computation.95 | convolution fusion | flops 141295616 | bytes 52465664 | tf_op jit(solution)/shard_map/ock,bczyx->bozyxk/dot_general | solution.py:108
  576.2 20.7 %copy.281 = f32[1,28,2,64,64,2,2]{1,6,4,5,3,2,0:T(2,128)} copy(f32[1,28,2,64,64,2,2]{4,1,6,5,3,2,0:T(8,128)} %bitcast.1075) | data formatting | bytes 7340032 | tf_op jit(solution)/shard_map/reshape | solution.py:109
  596.9 11.5 %copy.282 = f32[1,28,2,128,128]{4,1,3,2,0:T(8,128)} copy(f32[1,28,2,128,128]{1,4,3,2,0:T(8,128)} %bitcast.1073) | data formatting | bytes 7340032 | tf_op jit(solution)/shard_map/reshape | solution.py:110
  608.4 4.0 fusion.45
  (184 shorter events, 175.6 us)
Async XLA Ops:
  0.0 542.1 %copy-start = (bf16[28,56,4]{1,2,0:T(4,128)(2,1)S(1)}, bf16[28,56,4]{1,2,0:T(4,128)(2,1)}, u32[]{:S(2)}) copy-start(bf16[28,56,4]{1,2,0:T(4,128)(2,1)} %param.12) | copy-start | bytes 37636
  0.0 75.4 %copy-start.8 = (bf16[28,9]{0,1:T(8,128)(2,1)S(1)}, bf16[28,9]{0,1:T(8,128)(2,1)}, u32[]{:S(2)}) copy-start(bf16[28,9]{0,1:T(8,128)(2,1)} %param.9) | copy-start | bytes 1516
  175.5 7.4 %copy-start.2 = (bf16[1,28,2,128,1]{4,1,3,2,0:T(8,128)(2,1)S(1)}, bf16[1,28,2,128,1]{4,1,3,2,0:T(8,128)(2,1)}, u32[]{:S(2)}) copy-start(bf16[1,28,2,128,1]{4,1,3,2,0:T(8,128)(2,1)} %copy.246) | copy-start | bytes 43012
  175.5 7.4 %copy-start.3 = (bf16[1,28,2,128,1]{4,1,3,2,0:T(8,128)(2,1)S(1)}, bf16[1,28,2,128,1]{4,1,3,2,0:T(8,128)(2,1)}, u32[]{:S(2)}) copy-start(bf16[1,28,2,128,1]{4,1,3,2,0:T(8,128)(2,1)} %copy.247) | copy-start | bytes 43012
  176.6 45.0 %collective-permute-start = (bf16[1,28,1,130,130]{4,3,2,1,0:T(8,128)(2,1)S(1)}, bf16[1,28,1,130,130]{4,3,2,1,0:T(8,128)(2,1)S(1)}, u32[]{:S(2)}, u32[]{:S(2)}) collective-permute-start(bf16[1,28,1,130,130]{4,3,2,1,0:T(8,128)(2,1)S(1)} %copy.251), channel_id=1, source_target_pairs={{0,32},{32,64},{64,96},{1,33},{33,65},{65,97},{2,34},{34,66},{66,9... | collective-permute-start | bytes 2839208 | tf_op jit(solution)/shard_map/ppermute | solution.py:15
  181.0 12.1 %copy-start.7 = (bf16[28,28,27]{1,0,2:T(8,128)(2,1)S(1)}, bf16[28,28,27]{1,0,2:T(8,128)(2,1)}, u32[]{:S(2)}) copy-start(bf16[28,28,27]{1,0,2:T(8,128)(2,1)} %param.10) | copy-start | bytes 127012
  181.1 45.6 %collective-permute-start.1 = (bf16[1,28,1,130,130]{4,3,2,1,0:T(8,128)(2,1)S(1)}, bf16[1,28,1,130,130]{4,3,2,1,0:T(8,128)(2,1)S(1)}, u32[]{:S(2)}, u32[]{:S(2)}) collective-permute-start(bf16[1,28,1,130,130]{4,3,2,1,0:T(8,128)(2,1)S(1)} %copy.256), channel_id=1, source_target_pairs={{32,0},{64,32},{96,64},{33,1},{65,33},{97,65},{34,2},{66,34},{98,6... | collective-permute-start | bytes 2839208 | tf_op jit(solution)/shard_map/ppermute | solution.py:17
  247.1 46.0 %copy-start.1 = (bf16[1,28,3,130,130]{4,1,3,2,0:T(8,128)(2,1)}, bf16[1,28,3,130,130]{4,1,3,2,0:T(8,128)(2,1)S(1)}, u32[]{:S(2)}) copy-start(bf16[1,28,3,130,130]{4,1,3,2,0:T(8,128)(2,1)S(1)} %get-tuple-element.14) | copy-start | bytes 8517604
  451.1 4.1 copy-start.4
  451.1 4.1 copy-start.5
  455.1 2.5 copy-start.6
  476.9 14.0 %collective-permute-start.2 = (bf16[1,28,1,66,66]{4,3,2,1,0:T(8,128)(2,1)S(1)}, bf16[1,28,1,66,66]{4,3,2,1,0:T(8,128)(2,1)S(1)}, u32[]{:S(2)}, u32[]{:S(2)}) collective-permute-start(bf16[1,28,1,66,66]{4,3,2,1,0:T(8,128)(2,1)S(1)} %copy.273), channel_id=1, source_target_pairs={{0,32},{32,64},{64,96},{1,33},{33,65},{65,97},{2,34},{34,66},{66,9... | collective-permute-start | bytes 731816 | tf_op jit(solution)/shard_map/ppermute | solution.py:15
  480.1 14.8 %collective-permute-start.3 = (bf16[1,28,1,66,66]{4,3,2,1,0:T(8,128)(2,1)S(1)}, bf16[1,28,1,66,66]{4,3,2,1,0:T(8,128)(2,1)S(1)}, u32[]{:S(2)}, u32[]{:S(2)}) collective-permute-start(bf16[1,28,1,66,66]{4,3,2,1,0:T(8,128)(2,1)S(1)} %copy.278), channel_id=1, source_target_pairs={{32,0},{64,32},{96,64},{33,1},{65,33},{97,65},{34,2},{66,34},{98,6... | collective-permute-start | bytes 731816 | tf_op jit(solution)/shard_map/ppermute | solution.py:17
  596.9 11.5 %copy-start.9 = (bf16[3,28]{1,0:T(4,128)(2,1)S(1)}, bf16[3,28]{1,0:T(4,128)(2,1)}, u32[]{:S(2)}) copy-start(bf16[3,28]{1,0:T(4,128)(2,1)} %param.13) | copy-start | bytes 508
where the time goes:
time: 623 us; the launch traced here: 614 us
  matrix products  222 us (36%)
  blocking collectives  211 us (34%)
  local copies, waits for them, and re-layouts  84.2 us (14%)
  other arithmetic  70.6 us (11%)
  waiting for transfers between devices  15.4 us (2%)
  starting transfers between devices  9.56 us (2%)
    dot_general x53, matrix products, convolve(): jnp.einsum('oi,bizyx->bozyx', taps, window, preferred_element_type=jnp.fl...  182 us
    all_gather x3, blocking collectives, on_device(): lax.all_gather(parts[1], 'xy', axis=0, tiled=True)  71.8 us
    all_gather x3, blocking collectives, on_device(): lax.all_gather(parts[0], 'xy', axis=0, tiled=True)  70 us
    all_gather x3, blocking collectives, on_device(): lax.all_gather(parts[2], 'xy', axis=0, tiled=True)  69.2 us
    dot_general x1, matrix products, finish(): jnp.einsum('ock,bczyx->bozyxk', up_kernel, coarse, preferred_element_type...  34.1 us
    concatenate x2, other arithmetic, with_halo(): jnp.concatenate([lax.ppermute(tail, axis, [(i, (i + 1) % count) for i in...  23.8 us
    concatenate x5, other arithmetic, assemble(): return jnp.concatenate([upper, middle, lower], axis=3)  23.1 us
    reshape x1, local copies, waits for them, and re-layouts, finish(): upward = upward.reshape(blocks, -1, planes, height, width, 2, 2)  20.7 us
  transfers between devices with their start and end apart: 4, of which 4 were waited for; matrix products, arithmetic and copies ran while one was open for 7% of the time, Pallas kernels for 0%

commit v1 on v0

v1 whole, which is shorter than its diff:
```python
import jax
import jax.numpy as jnp
from jax import lax
from jax.experimental import pallas as pl
from jax.experimental.pallas import tpu as pltpu
from jax.sharding import PartitionSpec as P

F32 = jnp.float32
BF16 = jnp.bfloat16
PITCH = 40
LINES = 66
FIRST_OFF = 256.0
SKIP_OFF = 65536.0
VMEM = pl.BlockSpec(memory_space=pltpu.VMEM)
SMEM = pl.BlockSpec(memory_space=pltpu.SMEM)
NT = (((1,), (1,)), ((), ()))


def iota(shape, dim):
    return lax.broadcasted_iota(jnp.int32, shape, dim)


def dot(a, b):
    return jnp.dot(a, b, preferred_element_type=F32)


def dot_nt(a, b):
    return lax.dot_general(a, b, NT, preferred_element_type=F32)


def pack_kernel(nb, prev, own, nxt, slots, rows):
    slots[...] = jnp.zeros(slots.shape, BF16)
    rows[...] = jnp.zeros(rows.shape, F32)
    lane, line = iota((16, 128), 1), iota((16, 128), 0)
    edge = jnp.where(lane == jnp.where(line < 4, line, 120 + line), 1.0, 0.0).astype(BF16)
    for z in range(6):
        plane = (prev, own, nxt)[z // 2][z % 2]
        rows[0, pl.ds(z, 4, stride=8), :] = plane[0:16].astype(F32)[0:4]
        rows[1, pl.ds(z, 4, stride=8), :] = plane[112:128].astype(F32)[12:16]
        sides = dot_nt(edge, plane)
        rows[2, pl.ds(z, 4, stride=8), :] = sides[0:4]
        rows[3, pl.ds(z, 4, stride=8), :] = sides[4:8]
    for k, strip in enumerate((0, 1, 2, 3, 0, 0, 1, 1)):

        @pl.when(nb[0, k] >= 0)
        def _():
            slots[jnp.maximum(nb[0, k], 0)] = rows[strip].astype(BF16)


def weights_kernel(first, second, coarse, up, head, wf, ws, wc, wu, ht, taps2, tapsc, taps1, tapsh):
    lane = iota((32, 128), 1)
    turned = jnp.concatenate([second[...].astype(F32)] * 4, axis=0).T
    taps1[...] = turned
    for tap in range(27):
        fill = jnp.where((iota((4, 128), 0) == 0) & (iota((4, 128), 1) % 32 < 28), -SKIP_OFF, 0.0)
        taps2[tap * 32 : tap * 32 + 28, :] = taps1[pl.ds(tap, 28, stride=27), :]
        taps2[tap * 32 + 28 : tap * 32 + 32, :] = fill if tap == 13 else jnp.zeros((4, 128), F32)
    for z in range(4):
        for row in range(4):
            for col in range(4):
                block = (z * 2 + row // 2) * 8 + (col // 2) * 4 + (row % 2) * 2 + col % 2
                for half in range(2):
                    value = jnp.zeros((32, 128), F32)
                    for slot in range(4):
                        dz, dr, dc = z - half, row - slot // 2, col - slot % 2
                        if 0 <= dz < 3 and 0 <= dr < 3 and 0 <= dc < 3:
                            tap = dz * 9 + dr * 3 + dc
                            value = jnp.where(lane // 32 == slot, taps2[tap * 32 : tap * 32 + 32, :], value)
                    ws[block * 32 : block * 32 + 32, half * 128 : half * 128 + 128] = value.astype(BF16)
    taps1[...] = jnp.concatenate([coarse[...].astype(F32)] * 2, axis=0).T
    for tap in range(27):
        tapsc[tap * 32 : tap * 32 + 28, :] = taps1[pl.ds(tap, 28, stride=27), :]
        tapsc[tap * 32 + 28 : tap * 32 + 32, :] = jnp.zeros((4, 128), F32)
    for dy in range(3):
        for z in range(4):
            for col in range(4):
                block = (dy * 4 + z) * 4 + col
                for half in range(2):
                    value = jnp.zeros((32, 128), F32)
                    for slot in range(2):
                        dz, dc = z - slot, col - half
                        if 0 <= dz < 3 and 0 <= dc < 3:
                            tap = dz * 9 + dy * 3 + dc
                            value = jnp.where(lane // 64 == slot, tapsc[tap * 32 : tap * 32 + 32, :], value)
                    wc[block * 32 : block * 32 + 32, half * 128 : half * 128 + 128] = value.astype(BF16)
    taps1[0:256, :] = jnp.concatenate([up[...].astype(F32)] * 4, axis=0).T
    mixed = jnp.zeros((64, 128), F32)
    for tap in range(4):
        mixed = jnp.where(iota((64, 128), 1) // 32 == tap, taps1[pl.ds(tap, 64, stride=4), :], mixed)
    mixed = jnp.where(iota((64, 128), 0) < 56, mixed, 0.0).astype(BF16)
    nothing = jnp.zeros((64, 128), BF16)
    wu[0:64, 0:128] = mixed
    wu[0:64, 128:256] = nothing
    wu[64:128, 0:128] = nothing
    wu[64:128, 128:256] = mixed
    tapsh[...] = jnp.zeros(tapsh.shape, F32)
    tapsh[0:28, 0:9] = first[...].astype(F32)
    by_tap = jnp.concatenate([tapsh[0:32, :]] * 4, axis=0).T
    by_tap = jnp.concatenate([by_tap] * 3, axis=1)
    at, to = iota((256, 384), 0), iota((256, 384), 1)
    row = (at // 128) * 2 + (at // 8) % 2 - (to // 64) % 2
    col = (at // 16) % 8 - (to // 128) * 2 - (to // 32) % 2
    window = jnp.where((row >= 0) & (row < 3) & (col >= 0) & (col < 3), row * 3 + col, -1)
    spread = jnp.zeros((256, 384), F32)
    for tap in range(9):
        spread = jnp.where(window == tap, by_tap[tap : tap + 1, :], spread)
    off = jnp.where(to % 32 < 28, -FIRST_OFF, jnp.where(to % 32 == 28, 1.0, 0.0))
    off = jnp.where((window == 4) & (at % 8 == 6), off, 0.0)
    for z in range(6):
        wf[:, z * 384 : z * 384 + 384] = jnp.where(at % 8 == z, spread, off).astype(BF16)
    tapsh[...] = jnp.zeros(tapsh.shape, F32)
    tapsh[0:3, 0:28] = head[...].astype(F32)
    narrow = tapsh[0:8, :]
    wide = narrow
    for turn in (32, 64, 96):
        wide = wide + pltpu.roll(narrow, turn, 1)
    wide = jnp.concatenate([wide, wide], axis=1)
    at, to = iota((32, 256), 0), iota((32, 256), 1)
    fits = (at // 16 == (to // 32) % 2) & (at % 2 == (to // 64) % 2) & ((at // 2) % 2 == to // 128)
    value = jnp.zeros((32, 256), F32)
    for k in range(3):
        value = jnp.where(fits & ((at % 16) // 4 == k), wide[k : k + 1, :], value)
    ht[...] = value.astype(BF16)


def main_kernel(meta, prev, own, nxt, recv, wf, ws, wc, wu, ht, out, ext, strips, turned, shifted, taps, first, pooled, skip, flat, mixed):
    ext[...] = jnp.zeros(ext.shape, F32)
    side_lane = iota((32, 128), 1)
    plane_row = iota((32, 128), 0) % 8
    gone = jnp.where(plane_row == 6, 1.0, 0.0)

    def strip(k):
        have = meta[0, k] >= 0
        return jnp.where(have, recv[jnp.maximum(meta[0, k], 0)].astype(F32), gone)

    north, south, west, east = strip(0), strip(1), strip(2), strip(3)
    for start, middle, left, right in ((0, north, strip(4), strip(5)), (1056, south, strip(6), strip(7))):
        ext[0, start : start + 32, :] = middle
        ext[1, start : start + 32, :] = jnp.where(side_lane < 4, right, jnp.where(side_lane >= 124, left, 0.0))
    strips[0] = west
    strips[1] = east
    turned[...] = jnp.zeros(turned.shape, F32)
    for z in range(7):
        if z < 6:
            plane = (prev, own, nxt)[z // 2][z % 2]
            ext[0, pl.ds(32 + z, 128, stride=8), :] = plane.astype(F32)
        turned[0:4, :] = strips[1, pl.ds(z, 4, stride=8), :]
        turned[124:128, :] = strips[0, pl.ds(z, 4, stride=8), :]
        ext[1, pl.ds(32 + z, 128, stride=8), :] = turned[...].T

    for c in range(8):
        for part in range(4):
            rows = pl.ds(part * 272, 272)
            value = jnp.concatenate([ext[0, rows, :], ext[1, rows, :]], axis=1)
            if c != 4:
                value = pltpu.roll(value, (4 - c) % 256, 1)
            shifted[c, rows, :] = value.astype(BF16)

    pick = jnp.where((iota((PITCH, 256), 1) == 4 * iota((PITCH, 256), 0)) & (iota((PITCH, 256), 0) < 33), 1.0, 0.0)
    pick = pick.astype(BF16)

    def gather(t, _):
        lines = [
            shifted[c, pl.ds(pl.multiple_of(t * 32, 32) + 16 * h, 16), :] for h in range(2) for c in range(8)
        ]
        got = dot_nt(pick, jnp.concatenate(lines, axis=0))
        both = jnp.concatenate([got[:, 0:128], got[:, 128:256]], axis=0)
        taps[pl.ds(pl.multiple_of(t * 2 * PITCH, 2 * PITCH), 2 * PITCH), :] = both.astype(BF16)
        return 0

    lax.fori_loop(0, 34, gather, 0)

    def first_rows(base, count):
        below = taps[pl.ds(base + 32, count + 16), :][8 : count + 8]
        window = jnp.concatenate([taps[pl.ds(base, count), :], below], axis=1)
        for z in range(0, 6, 2):
            got = jnp.maximum(dot(window, wf[:, z * 384 : z * 384 + 768]), 0.0).astype(BF16)
            first[z, pl.ds(base, count), :] = got[:, 0:384]
            first[z + 1, pl.ds(base, count), :] = got[:, 384:768]

    def first_step(g, _):
        first_rows(pl.multiple_of(g * 240, 240), 240)
        return 0

    lax.fori_loop(0, 11, first_step, 0)
    first_rows(2640, 48)

    at, to = iota((256, 256), 0), iota((256, 256), 1)
    meets = (at // 128 == to // 128) & (at % 32 == to % 32)
    outside = ((meta[0, 8] == 0, False), (False, meta[0, 8] == 3))
    pools = []
    for p in range(2):
        scale = jnp.where(to < 128, jnp.where(outside[p][0], 0.0, 0.25), jnp.where(outside[p][1], 0.0, 0.25))
        pools.append([jnp.where(meets & ((to // 32) % 2 == par), scale, 0.0).astype(BF16) for par in range(2)])

    def skip_step(g, _):
        base = pl.multiple_of(g * 240, 240)
        lines = [
            (first[z, pl.ds(base, 240), :], first[z, pl.ds(base + 32, 256), :][8:248]) for z in range(6)
        ]
        for p in range(2):
            mean = None
            for par in range(2):
                total = None
                for z in range(4):
                    for dy in range(2):
                        window = lines[2 * p + z][dy][:, par * 128 : par * 128 + 256]
                        at = (z * 2 + dy) * 256
                        term = dot(window, ws[at : at + 256, :])
                        total = term if total is None else total + term
                total = jnp.maximum(total, 0.0)
                term = dot(total.astype(BF16), pools[p][par])
                mean = term if mean is None else mean + term
                inner = total[:, 128:256] if p == 0 else total[:, 0:128]
                if par == 0:
                    inner = pltpu.roll(inner, 239, 0)
                for y in range(6):
                    rows = pl.ds(pl.multiple_of(g * 192, 192) + y * 32, 32)
                    skip[1 - par, rows, p * 128 : p * 128 + 128] = inner[y * PITCH : y * PITCH + 32].astype(BF16)
            after = pltpu.roll(mean, 239, 0)
            mean = jnp.where(iota((240, 256), 1) % 128 < 64, mean, after)
            for y in range(6):
                rows = pl.ds(pl.multiple_of(g * 192, 192) + y * 32, 32)
                pooled[p, rows, :] = mean[y * PITCH : y * PITCH + 32].astype(BF16)
        return 0

    lax.fori_loop(0, 11, skip_step, 0)

    def last_step(g, _):
        base = pl.multiple_of(g * 256, 256)
        total = None
        for dy in range(3):
            for p in range(2):
                at = (dy * 2 + p) * 256
                term = dot(pooled[p, pl.ds(base + dy * 32, 256), :], wc[at : at + 256, :])
                total = term if total is None else total + term
        coarse = jnp.maximum(total, 0.0).astype(BF16)
        joined = []
        for side in range(2):
            upward = dot(coarse[:, side * 128 : side * 128 + 128], wu[...])
            upward = upward + skip[side, pl.ds(base + 32, 256), :].astype(F32)
            joined.append(jnp.maximum(upward, 0.0).astype(BF16))
        for half in range(2):
            lines = [joined[side][y * 32 : y * 32 + 32] for y in range(half * 4, half * 4 + 4) for side in range(2)]
            logits = dot_nt(ht[...], jnp.concatenate(lines, axis=0))
            high = logits.astype(BF16)
            low = (logits - high.astype(F32)).astype(BF16)
            for pair in range(2):
                rows = pl.ds(pl.multiple_of(g * 64, 64) + (half * 2 + pair) * 16, 16)
                lanes = slice(pair * 128, pair * 128 + 128)
                flat[rows, 0:128] = high[0:16, lanes]
                flat[rows, 128:256] = low[0:16, lanes]
                flat[rows, 256:384] = high[16:32, lanes]
                flat[rows, 384:512] = low[16:32, lanes]
        return 0

    lax.fori_loop(0, 8, last_step, 0)

    at, to = iota((512, 256), 0), iota((512, 256), 1)
    column = 4 * (at % 32) + 2 * ((at // 32) % 2) + at // 256
    place = jnp.where(((at // 64) % 2 == to // 128) & (column == to % 128), 1.0, 0.0).astype(BF16)
    logits = dot(flat[...], place)
    mixed[0] = logits[:, 0:128]
    mixed[1] = logits[:, 128:256]
    for k in range(3):
        for z in range(2):
            for line in range(4):
                row = k * 4 + z * 2 + line % 2
                out[0, k, z, pl.ds(line, 32, stride=4), :] = mixed[line // 2, pl.ds(row, 32, stride=16), :]


def on_device(em_volume, neighbours, first_kernel, second_kernel, coarse_kernel, up_kernel, head_kernel):
    own = em_volume[0]
    steps = lax.axis_size("gz")
    prev = lax.ppermute(own, "gz", [(i, i + 1) for i in range(steps - 1)])
    nxt = lax.ppermute(own, "gz", [(i + 1, i) for i in range(steps - 1)])
    limit = pltpu.CompilerParams(vmem_limit_bytes=56 * 2**20)

    second = jnp.pad(second_kernel.reshape(28, 756), ((0, 4), (0, 12)))
    coarse = jnp.pad(coarse_kernel.reshape(56, 756), ((0, 8), (0, 12)))
    up = jnp.pad(up_kernel.reshape(28, 224), ((0, 4), (0, 32)))
    shapes = [(256, 2304), (2048, 256), (1536, 256), (128, 256), (32, 256)]
    weights = pl.pallas_call(
        weights_kernel,
        out_shape=[jax.ShapeDtypeStruct(s, BF16) for s in shapes],
        in_specs=[VMEM] * 5,
        out_specs=[VMEM] * 5,
        scratch_shapes=[
            pltpu.VMEM((864, 128), F32),
            pltpu.VMEM((864, 128), F32),
            pltpu.VMEM((768, 128), F32),
            pltpu.VMEM((32, 128), F32),
        ],
        compiler_params=limit,
        cost_estimate=pl.CostEstimate(flops=10**8, bytes_accessed=4 * 10**6, transcendentals=0),
        name="weights",
    )(first_kernel, second, coarse, up, head_kernel)

    slots = pl.pallas_call(
        pack_kernel,
        out_shape=jax.ShapeDtypeStruct((32, 32, 128), BF16),
        in_specs=[SMEM] + [VMEM] * 3,
        out_specs=VMEM,
        scratch_shapes=[pltpu.VMEM((4, 32, 128), F32)],
        compiler_params=limit,
        name="pack",
    )(neighbours, prev, own, nxt)
    recv = lax.all_to_all(slots, "xy", 0, 0, tiled=True)

    place = jnp.full((1, 1), lax.axis_index("gz"), jnp.int32)
    meta = jnp.concatenate([neighbours, place], axis=1)
    return pl.pallas_call(
        main_kernel,
        out_shape=jax.ShapeDtypeStruct((1, 3, 2, 128, 128), F32),
        in_specs=[SMEM] + [VMEM] * 9,
        out_specs=VMEM,
        scratch_shapes=[
            pltpu.VMEM((2, 1088, 128), F32),
            pltpu.VMEM((2, 32, 128), F32),
            pltpu.VMEM((128, 128), F32),
            pltpu.VMEM((8, 1088, 256), BF16),
            pltpu.VMEM((2736, 128), BF16),
            pltpu.VMEM((6, 2688, 384), BF16),
            pltpu.VMEM((2, LINES * 32, 256), BF16),
            pltpu.VMEM((2, LINES * 32, 256), BF16),
            pltpu.VMEM((512, 512), BF16),
            pltpu.VMEM((2, 512, 128), F32),
        ],
        compiler_params=limit,
        name="layers",
    )(meta, prev, own, nxt, recv, *weights)


def solution(mesh):
    placed = (P("xy", "gz", None, None), P("xy", None), P(), P(), P(), P(), P())
    return jax.shard_map(
        on_device,
        mesh=mesh,
        in_specs=placed,
        out_specs=P("xy", None, "gz", None, None),
        check_vma=False,
    )
```

time: 623 us -> 72.9 us (0.12); the launches traced: 614 us -> 72.2 us
  matrix products: 222 us -> 0 us
  blocking collectives: 211 us -> 0 us
  local copies, waits for them, and re-layouts: 84.2 us -> 7.75 us
  other arithmetic: 70.6 us -> 0.58 us
  Pallas kernels: 0 us -> 46.1 us
  waiting for transfers between devices: 15.4 us -> 1.61 us
  starting transfers between devices: 9.56 us -> 16.1 us
    dot_general x62 -> x0, matrix products: 222 us -> none  [the longest x53 182 us: convolve(): jnp.einsum('oi,bizyx->bozyx', taps, window, preferred_element_type=jnp.fl...]
    all_gather x9 -> x0, blocking collectives: 211 us -> none  [the longest x3 71.8 us: on_device(): lax.all_gather(parts[1], 'xy', axis=0, tiled=True)]
    concatenate x9 -> x1, other arithmetic: 47.1 us -> 0.58 us  [on_device(): meta = jnp.concatenate([neighbours, place], axis=1)]
    pallas_call x0 -> x3, Pallas kernels: none -> 46.1 us  [the longest x1 40.8 us: on_device(): pl.pallas_call(main_kernel, out_shape=jax.ShapeDtypeStruct((1, 3, 2, 128,...]
    reshape x2 -> x4, local copies, waits for them, and re-layouts: 32.2 us -> 1.86 us  [the longest x2 1.49 us: on_device(): coarse = jnp.pad(coarse_kernel.reshape(56, 756), ((0, 8), (0, 12)))]
    slice x17 -> x0, local copies, waits for them, and re-layouts: 20.4 us -> none  [the longest x6 10.8 us: exports(): features[:, :, :, :, :rim]]
    reduce_sum x1 -> x0, other arithmetic: 17.7 us -> none  [pool(): return (jnp.sum(grid, axis=(4, 6)) * 0.25).astype(jnp.bfloat16)]
    ppermute x4 -> x2, waiting for transfers between devices: 15.4 us -> 1.61 us  [the longest x1 1.61 us: on_device(): prev = lax.ppermute(own, 'gz', [(i, i + 1) for i in range(steps - 1)])]
  transfers between devices with their start and end apart: 4 -> 3, of which waited for: 4 -> 1; matrix products, arithmetic and copies ran while one was open for 7% -> 10% of each run, Pallas kernels for 0% -> 5%
where the time goes in v1:
time: 72.9 us; the launch traced here: 72.2 us
  Pallas kernels  46.1 us (63%)
  starting transfers between devices  16.1 us (22%)
  local copies, waits for them, and re-layouts  7.75 us (11%)
  waiting for transfers between devices  1.61 us (2%)
    pallas_call x1, Pallas kernels, on_device(): pl.pallas_call(main_kernel, out_shape=jax.ShapeDtypeStruct((1, 3, 2, 128,...  40.8 us
    all_to_all x1, starting transfers between devices, on_device(): recv = lax.all_to_all(slots, 'xy', 0, 0, tiled=True)  10.2 us
    ppermute x1, starting transfers between devices, on_device(): prev = lax.ppermute(own, 'gz', [(i, i + 1) for i in range(steps - 1)])  4.58 us
    unnamed x15, local copies, waits for them, and re-layouts  4.01 us
    pallas_call x1, Pallas kernels, on_device(): pl.pallas_call(weights_kernel, out_shape=[jax.ShapeDtypeStruct(s, BF16) f...  3.44 us
    pallas_call x1, Pallas kernels, on_device(): pl.pallas_call(pack_kernel, out_shape=jax.ShapeDtypeStruct((32, 32, 128),...  1.84 us
    ppermute x1, waiting for transfers between devices, on_device(): prev = lax.ppermute(own, 'gz', [(i, i + 1) for i in range(steps - 1)])  1.61 us
    reshape x2, local copies, waits for them, and re-layouts, on_device(): coarse = jnp.pad(coarse_kernel.reshape(56, 756), ((0, 8), (0, 12)))  1.49 us
  transfers between devices with their start and end apart: 3, of which 1 were waited for; matrix products, arithmetic and copies ran while one was open for 10% of the time, Pallas kernels for 5%

profile of v1, /device:TPU:1, one launch (start us, length us, event | category | flops | bytes accessed | tf_op | source)
XLA Modules:
  0.0 72.2 jit_solution(11160229657145061844)
XLA Ops:
  0.0 0.0 copy-start.3
  0.0 0.0 copy-start.4
  0.0 1.4 %collective-permute-start.1 = (bf16[2,128,128]{2,1,0:T(8,128)(2,1)}, bf16[2,128,128]{2,1,0:T(8,128)(2,1)S(1)}, u32[]{:S(2)}, u32[]{:S(2)}) collective-permute-start(bf16[2,128,128]{2,1,0:T(8,128)(2,1)} %bitcast.3), channel_id=1, source_target_pairs={{32,0},{64,32},{96,64},{33,1},{65,33},{97,65},{34,2},{66,34},{98,6... | collective-permute-start | bytes 196616 | tf_op jit(solution)/shard_map/ppermute | solution.py:276
  1.4 4.6 %collective-permute-start = (bf16[2,128,128]{2,1,0:T(8,128)(2,1)}, bf16[2,128,128]{2,1,0:T(8,128)(2,1)S(1)}, u32[]{:S(2)}, u32[]{:S(2)}) collective-permute-start(bf16[2,128,128]{2,1,0:T(8,128)(2,1)} %bitcast.4), channel_id=1, source_target_pairs={{0,32},{32,64},{64,96},{1,33},{33,65},{65,97},{2,34},{34,66},{66,9... | collective-permute-start | bytes 196616 | tf_op jit(solution)/shard_map/ppermute | solution.py:275
  6.0 0.0 collective-permute-done.1.nxt
  6.0 0.0 copy-start.1
  6.0 1.6 %collective-permute-done.prev = bf16[2,128,128]{2,1,0:T(8,128)(2,1)S(1)} collective-permute-done((bf16[2,128,128]{2,1,0:T(8,128)(2,1)}, bf16[2,128,128]{2,1,0:T(8,128)(2,1)S(1)}, u32[]{:S(2)}, u32[]{:S(2)}) %collective-permute-start) | collective-permute-done | bytes 65568 | tf_op jit(solution)/shard_map/ppermute | solution.py:275
  7.6 0.0 copy-done.1
  7.6 0.0 copy-start.2
  7.6 0.6 copy-done.2
  8.3 1.8 %pack.1 = bf16[32,32,128]{2,1,0:T(8,128)(2,1)} custom-call(s32[1,8]{1,0:T(1,128)} %nb.1, bf16[2,128,128]{2,1,0:T(8,128)(2,1)} %copy-done.2, bf16[2,128,128]{2,1,0:T(8,128)(2,1)} %bitcast.5, bf16[2,128,128]{2,1,0:T(8,128)(2,1)} %copy-done.1), custom_call_target="tpu_custom_call" | custom-call | tf_op jit(solution)/shard_map/pack/pallas_call | solution.py:299
  10.1 10.2 %all-to-all-start = ((bf16[32,32,128]{2,1,0:T(8,128)(2,1)}), bf16[32,32,128]{2,1,0:T(8,128)(2,1)S(1)}, u32[]{:S(2)}, u32[]{:S(2)}) async-start(bf16[32,32,128]{2,1,0:T(8,128)(2,1)} %pack.1), calls=%async_computation | async-start | bytes 524288 | tf_op jit(solution)/shard_map/all_to_all | solution.py:308
  20.3 1.4 %copy.17.first = bf16[28,9]{1,0:T(8,128)(2,1)} copy(bf16[28,9]{0,1:T(8,128)(2,1)} %param.9) | data formatting | bytes 1008 | tf_op args[2]
  21.7 0.9 %copy.15 = bf16[28,56,4]{0,2,1:T(4,128)(2,1)S(1)} copy(bf16[28,56,4]{1,2,0:T(4,128)(2,1)} %param.12) | data formatting | bytes 25088 | tf_op args[5]
  22.6 0.1 copy.16
  22.6 0.0 copy-done.3
  22.7 0.4 copy.12
  23.1 0.0 copy-start.5
  23.1 0.3 reshape.9
  23.3 0.6 pad.14.up
  23.9 0.6 pad.12.second
  24.6 0.0 copy-done.4
  24.6 0.9 %copy.18 = bf16[56,28,27]{2,1,0:T(8,128)(2,1)S(1)} copy(bf16[56,28,27]{0,1,2:T(8,128)(2,1)S(1)} %copy-done.4) | data formatting | bytes 169344 | tf_op jit(solution)/shard_map/reshape | solution.py:280
  25.4 0.6 reshape.12
  26.1 0.7 pad.13.coarse
  26.7 3.4 %weights.1 = (bf16[256,2304]{1,0:T(8,128)(2,1)}, bf16[2048,256]{1,0:T(8,128)(2,1)}, bf16[1536,256]{1,0:T(8,128)(2,1)}, bf16[128,256]{1,0:T(8,128)(2,1)}, bf16[32,256]{1,0:T(8,128)(2,1)}) custom-call(bf16[28,9]{1,0:T(8,128)(2,1)} %copy.17.first, bf16[32,768]{1,0:T(8,128)(2,1)} %pad.12.second, bf16[64,768]{1,0:T(8,128)(2,1)} %pad.13.coarse, ...), custom_call_target="tpu_custom_call" | custom-call | flops 100000000 | bytes 4000000 | tf_op jit(solution)/shard_map/weights/pallas_call | solution.py:283
  30.2 0.0 copy-done.5
  30.2 0.6 pad_add_fusion.meta
  30.8 0.0 all-to-all-done.recv
  30.8 0.0 copy-start
  30.8 0.7 copy-done
  31.5 40.8 %layers.1 = f32[1,3,2,128,128]{4,3,2,1,0:T(8,128)} custom-call(s32[1,9]{1,0:T(1,128)} %pad_add_fusion.meta, bf16[2,128,128]{2,1,0:T(8,128)(2,1)} %copy-done.2, bf16[2,128,128]{2,1,0:T(8,128)(2,1)} %bitcast.6, bf16[2,128,128]{2,1,0:T(8,128)(2,1)} %copy-done.1, bf16[32,32,128]{2,1,0:T(8,128)(2,1)} %copy-done, bf16[256,2304]{1,0:T(8,128)(2,1)} %get-tuple-element.10.wf, ...), custom_call_target="tpu_custom_call" | custom-call | tf_op jit(solution)/shard_map/layers/pallas_call | solution.py:312
Async XLA Ops:
  0.0 22.6 %copy-start.3 = (bf16[28,28,27]{1,0,2:T(8,128)(2,1)S(1)}, bf16[28,28,27]{1,0,2:T(8,128)(2,1)}, u32[]{:S(2)}) copy-start(bf16[28,28,27]{1,0,2:T(8,128)(2,1)} %param.10) | copy-start | bytes 127012
  0.0 24.6 %copy-start.4 = (bf16[56,28,27]{0,1,2:T(8,128)(2,1)S(1)}, bf16[56,28,27]{0,1,2:T(8,128)(2,1)}, u32[]{:S(2)}) copy-start(bf16[56,28,27]{0,1,2:T(8,128)(2,1)} %param.11) | copy-start | bytes 254020
  0.0 6.0 %collective-permute-start.1 = (bf16[2,128,128]{2,1,0:T(8,128)(2,1)}, bf16[2,128,128]{2,1,0:T(8,128)(2,1)S(1)}, u32[]{:S(2)}, u32[]{:S(2)}) collective-permute-start(bf16[2,128,128]{2,1,0:T(8,128)(2,1)} %bitcast.3), channel_id=1, source_target_pairs={{32,0},{64,32},{96,64},{33,1},{65,33},{97,65},{34,2},{66,34},{98,6... | collective-permute-start | bytes 196616 | tf_op jit(solution)/shard_map/ppermute | solution.py:276
  1.4 6.2 %collective-permute-start = (bf16[2,128,128]{2,1,0:T(8,128)(2,1)}, bf16[2,128,128]{2,1,0:T(8,128)(2,1)S(1)}, u32[]{:S(2)}, u32[]{:S(2)}) collective-permute-start(bf16[2,128,128]{2,1,0:T(8,128)(2,1)} %bitcast.4), channel_id=1, source_target_pairs={{0,32},{32,64},{64,96},{1,33},{33,65},{65,97},{2,34},{34,66},{66,9... | collective-permute-start | bytes 196616 | tf_op jit(solution)/shard_map/ppermute | solution.py:275
  6.0 1.6 %copy-start.1 = (bf16[2,128,128]{2,1,0:T(8,128)(2,1)}, bf16[2,128,128]{2,1,0:T(8,128)(2,1)S(1)}, u32[]{:S(2)}) copy-start(bf16[2,128,128]{2,1,0:T(8,128)(2,1)S(1)} %collective-permute-done.1.nxt) | copy-start | bytes 196612
  7.6 0.6 copy-start.2
  10.1 20.6 %all-to-all-start = ((bf16[32,32,128]{2,1,0:T(8,128)(2,1)}), bf16[32,32,128]{2,1,0:T(8,128)(2,1)S(1)}, u32[]{:S(2)}, u32[]{:S(2)}) async-start(bf16[32,32,128]{2,1,0:T(8,128)(2,1)} %pack.1), calls=%async_computation | async-start | bytes 524288 | tf_op jit(solution)/shard_map/all_to_all | solution.py:308
  23.1 7.1 %copy-start.5 = (s32[1,8]{1,0:T(1,128)S(1)}, s32[1,8]{1,0:T(1,128)}, u32[]{:S(2)}) copy-start(s32[1,8]{1,0:T(1,128)} %nb.1) | copy-start | bytes 100
  30.8 0.7 copy-start

commit v2 on v1

v2 whole, which is shorter than its diff:
```python
import jax
import jax.numpy as jnp
from jax import lax
from jax.experimental import pallas as pl
from jax.experimental.pallas import tpu as pltpu
from jax.sharding import PartitionSpec as P

F32 = jnp.float32
BF16 = jnp.bfloat16
LINES = 66
FIRST_LINES, SKIP_LINES, LAST_LINES = 22, 22, 32
FIRST_OFF = 256.0
SKIP_OFF = 65536.0
VMEM = pl.BlockSpec(memory_space=pltpu.VMEM)
SMEM = pl.BlockSpec(memory_space=pltpu.SMEM)
NT = (((1,), (1,)), ((), ()))


def iota(shape, dim):
    return lax.broadcasted_iota(jnp.int32, shape, dim)


def dot(a, b):
    return jnp.dot(a, b, preferred_element_type=F32)


def dot_nt(a, b):
    return lax.dot_general(a, b, NT, preferred_element_type=F32)


def pack_kernel(nb, prev, own, nxt, slots, rows):
    slots[...] = jnp.zeros(slots.shape, BF16)
    lane, line = iota((16, 128), 1), iota((16, 128), 0)
    edge = jnp.where((lane == jnp.where(line < 4, line, 120 + line)) & (line < 8), 1.0, 0.0).astype(BF16)
    planes = jnp.concatenate([ref[z] for ref in (prev, own, nxt) for z in range(2)], axis=0)
    sides = dot_nt(edge, planes)
    for z in range(6):
        at = slice(4 * z, 4 * z + 4)
        rows[0, at, :] = planes[z * 128 : z * 128 + 16].astype(F32)[0:4]
        rows[1, at, :] = planes[z * 128 + 112 : z * 128 + 128].astype(F32)[12:16]
        rows[2, at, :] = sides[0:4, z * 128 : z * 128 + 128]
        rows[3, at, :] = sides[4:8, z * 128 : z * 128 + 128]
    for k, strip in enumerate((0, 1, 2, 3, 2, 3, 2, 3)):

        @pl.when(nb[0, k] >= 0)
        def _():
            slots[jnp.maximum(nb[0, k], 0)] = rows[strip].astype(BF16)


def weights_kernel(first, second, coarse, up, head, wf, ws, wc, wu, wh, taps2, tapsc, part, ups):
    lane = iota((32, 128), 1)
    part[...] = jnp.zeros(part.shape, F32)
    for four in range(7):
        value = jnp.zeros((32, 128), F32)
        for tap in range(4 * four, min(4 * four + 4, 27)):
            part[0:28, 0:28] = second[tap].astype(F32)
            turn = (tap % 4) * 32
            value = value + (pltpu.roll(part[0:32, :], turn, 1) if turn else part[0:32, :])
        turned = jnp.concatenate([value] * 4, axis=0).T
        taps2[four * 128 : four * 128 + 128, :] = turned
    fill = jnp.where(iota((1, 128), 1) % 32 < 28, -SKIP_OFF, 0.0)
    taps2[13 * 32 + 28 : 13 * 32 + 29, :] = fill
    for z in range(4):
        for row in range(4):
            for col in range(4):
                block = (z * 2 + row // 2) * 8 + (col // 2) * 4 + (row % 2) * 2 + col % 2
                for half in range(2):
                    value = jnp.zeros((32, 128), F32)
                    for slot in range(4):
                        dz, dr, dc = z - half, row - slot // 2, col - slot % 2
                        if 0 <= dz < 3 and 0 <= dr < 3 and 0 <= dc < 3:
                            tap = dz * 9 + dr * 3 + dc
                            value = jnp.where(lane // 32 == slot, taps2[tap * 32 : tap * 32 + 32, :], value)
                    ws[block * 32 : block * 32 + 32, half * 128 : half * 128 + 128] = value.astype(BF16)
    part[...] = jnp.zeros(part.shape, F32)
    for tap in range(27):
        part[0:28, 0:56] = coarse[tap].astype(F32)
        tapsc[tap * 32 : tap * 32 + 32, :] = part[0:32, :] + pltpu.roll(part[0:32, :], 64, 1)
    for dy in range(3):
        for z in range(4):
            for col in range(4):
                block = (dy * 4 + z) * 4 + col
                for half in range(2):
                    value = jnp.zeros((32, 128), F32)
                    for slot in range(2):
                        dz, dc = z - slot, col - half
                        if 0 <= dz < 3 and 0 <= dc < 3:
                            tap = dz * 9 + dy * 3 + dc
                            value = jnp.where(lane // 64 == slot, tapsc[tap * 32 : tap * 32 + 32, :], value)
                    wc[block * 32 : block * 32 + 32, half * 128 : half * 128 + 128] = value.astype(BF16)
    part[...] = jnp.zeros(part.shape, F32)
    ups[...] = jnp.zeros(ups.shape, F32)
    ups[:, 0:4, 0:56] = up[...].astype(F32)
    for channel in range(28):
        part[pl.ds(channel, 4, stride=32), :] = ups[channel, 0:4, :]
    mixed = part[...].T[0:64].astype(BF16)
    nothing = jnp.zeros((64, 128), BF16)
    wu[0:64, 0:128] = mixed
    wu[0:64, 128:256] = nothing
    wu[64:128, 0:128] = nothing
    wu[64:128, 128:256] = mixed
    part[...] = jnp.zeros(part.shape, F32)
    part[0:9, 0:28] = first[...].astype(F32)
    by_tap = part[0:16, :]
    by_tap = by_tap + pltpu.roll(by_tap, 32, 1)
    by_tap = by_tap + pltpu.roll(by_tap, 64, 1)
    by_tap = jnp.concatenate([by_tap] * 3, axis=1)
    at, to = iota((256, 384), 0), iota((256, 384), 1)
    row = (at // 128) * 2 + at % 2 - (to // 64) % 2
    col = (at // 2) % 8 - (to // 128) * 2 - (to // 32) % 2
    plane = (at // 16) % 8
    window = jnp.where((row >= 0) & (row < 3) & (col >= 0) & (col < 3), row * 3 + col, -1)
    spread = jnp.zeros((256, 384), F32)
    for tap in range(9):
        spread = jnp.where(window == tap, by_tap[tap : tap + 1, :], spread)
    off = jnp.where(to % 32 < 28, -FIRST_OFF, jnp.where(to % 32 == 28, 1.0, 0.0))
    off = jnp.where((window == 4) & (plane == 6), off, 0.0)
    for z in range(6):
        wf[:, z * 384 : z * 384 + 384] = jnp.where(plane == z, spread, off).astype(BF16)
    part[...] = jnp.zeros(part.shape, F32)
    part[0:3, 0:28] = head[...].astype(F32)
    by_map = part[...].T
    by_map = jnp.concatenate([by_map[0:32]] * 8, axis=0)
    at, to = iota((256, 128), 0), iota((256, 128), 1)
    fits = ((to // 16) % 2 == (at // 32) % 2) & (to % 2 == (at // 64) % 2) & ((to // 2) % 2 == at // 128)
    value = jnp.zeros((256, 128), F32)
    for k in range(3):
        value = jnp.where(fits & ((to % 16) // 4 == k), by_map[:, k : k + 1], value)
    for block in range(4):
        wh[block * 256 : block * 256 + 256, :] = jnp.where(to // 32 == block, value, 0.0).astype(BF16)


def main_kernel(meta, prev, own, nxt, recv, wf, ws, wc, wu, wh, out, ext, strips, turned, taps, edge_taps, first, edge_mean, pooled, skip, high, low, mixed):
    strips[...] = jnp.zeros(strips.shape, F32)
    for k in range(8):
        have = meta[0, k] >= 0
        strips[k, 4:28, :] = jnp.where(have, recv[jnp.maximum(meta[0, k], 0)].astype(F32), 0.0)
        strips[k, 28:32, :] = jnp.full((4, 128), jnp.where(have, 0.0, 1.0), F32)

    ext[...] = jnp.zeros(ext.shape, F32)
    for z in range(7):
        if z < 6:
            ext[z, 4:132, :] = (prev, own, nxt)[z // 2][z % 2].astype(F32)
        ext[z, 0:4, :] = strips[0, 4 * z + 4 : 4 * z + 8, :]
        ext[z, 132:136, :] = strips[1, 4 * z + 4 : 4 * z + 8, :]

    lane = iota((8, 128), 1)
    edge_taps[...] = jnp.zeros(edge_taps.shape, F32)
    for b in range(9):
        lines = [ext[z, 16 * b : 16 * b + 16, :] for z in range(8)]
        turned[b, 8:136, :] = jnp.concatenate(lines, axis=0).T
        for start, sides, shift in ((0, (4, 2, 6), 0), (136, (5, 3, 7), 4)):
            value = jnp.zeros((8, 128), F32)
            for z in range(7):
                rows = slice(4 * z + shift, 4 * z + shift + 8)
                line = strips[sides[1], rows, :]
                if b == 0:
                    line = jnp.where(lane >= 124, strips[sides[0], rows, :], line)
                if b == 8:
                    line = jnp.where(lane < 4, strips[sides[2], rows, :], jnp.where(lane >= 124, line, 0.0))
                turn = (16 * z - 16 * b + 4) % 128
                value = jnp.where(lane // 16 == z, pltpu.roll(line, turn, 1) if turn else line, value)
            turned[b, start : start + 8, :] = value
        parts = [
            jnp.concatenate(
                [turned[b, pl.ds(6 + c, 32, stride=4), :], turned[b, pl.ds(2 + c, 2, stride=132), :]], axis=0
            )
            for c in range(8)
        ]
        for bit in (1, 2, 4):
            side = (iota((34, 128), 1) // (2 * bit)) % 2 == 0
            for a in range(8):
                if not a & bit:
                    one, two = parts[a], parts[a + bit]
                    parts[a] = jnp.where(side, one, pltpu.roll(two, 2 * bit, 1))
                    parts[a + bit] = jnp.where(side, pltpu.roll(one, 128 - 2 * bit, 1), two)
        for y in range(8):
            at = 8 * b + y
            if at < 68:
                taps[at * 32 : at * 32 + 32, :] = parts[y][0:32].astype(BF16)
                edge_taps[0, at : at + 1, :] = parts[y][32:33]
                edge_taps[1, at : at + 1, :] = parts[y][33:34]

    at, to = iota((256, 256), 0), iota((256, 256), 1)
    meets = (at // 128 == to // 128) & (at % 32 == to % 32)
    outside = ((meta[0, 8] == 0, False), (False, meta[0, 8] == 3))
    pools = []
    for p in range(2):
        scale = jnp.where(to < 128, jnp.where(outside[p][0], 0.0, 0.25), jnp.where(outside[p][1], 0.0, 0.25))
        pools.append([jnp.where(meets & ((to // 32) % 2 != par), scale, 0.0).astype(BF16) for par in range(2)])

    def add_dots(pairs):
        total = None
        for a, b in pairs:
            term = dot(a, b)
            total = term if total is None else total + term
        return total

    windows = []
    for side in range(2):
        lines = [edge_taps[side, pl.ds(dy, 80), :].astype(BF16) for dy in range(3)]
        windows += [jnp.concatenate(lines[dy : dy + 2], axis=1) for dy in range(2)]
    edges = jnp.maximum(dot(jnp.concatenate(windows, axis=0), wf[...]), 0.0).astype(BF16)
    for p in range(2):
        pairs = []
        for z in range(4):
            for dy in range(2):
                lanes = (2 * p + z) * 384
                west = edges[dy * 80 : dy * 80 + 80, lanes + 128 : lanes + 384]
                east = edges[160 + dy * 80 : 240 + dy * 80, lanes : lanes + 256]
                pairs.append((jnp.concatenate([west, east], axis=0), ws[(z * 2 + dy) * 256 : (z * 2 + dy) * 256 + 256, :]))
        value = jnp.maximum(add_dots(pairs), 0.0).astype(BF16)
        edge_mean[p, 0] = dot(value[0:80], pools[p][1])
        edge_mean[p, 1] = dot(value[80:160], pools[p][0])

    def first_rows(base, count):
        window = jnp.concatenate([taps[pl.ds(base, count), :], taps[pl.ds(base + 32, count), :]], axis=1)
        for n in range(0, 2304, 256):
            first[pl.ds(base, count), n : n + 256] = jnp.maximum(dot(window, wf[:, n : n + 256]), 0.0).astype(BF16)

    def first_step(g, _):
        first_rows(pl.multiple_of(g * (FIRST_LINES * 32), FIRST_LINES * 32), FIRST_LINES * 32)
        return 0

    lax.fori_loop(0, 66 // FIRST_LINES, first_step, 0)
    first_rows(2112, 32)

    def skip_step(g, _):
        count = SKIP_LINES * 32
        base = pl.multiple_of(g * count, count)
        group = (iota((count, 256), 1) // 32) % 4
        line_row, line_group = iota((32, 256), 0), (iota((32, 256), 1) // 32) % 4
        for p in range(2):
            values = []
            for par in range(2):
                pairs = []
                for z in range(4):
                    for dy in range(2):
                        lanes = (2 * p + z) * 384 + par * 128
                        at = (z * 2 + dy) * 256
                        pairs.append((first[pl.ds(base + dy * 32, count), lanes : lanes + 256], ws[at : at + 256, :]))
                value = jnp.maximum(add_dots(pairs), 0.0).astype(BF16)
                skip[par, pl.ds(base, count), p * 128 : p * 128 + 128] = value[:, 128 - p * 128 : 256 - p * 128]
                values.append(value)
            mean = add_dots([(values[0], pools[p][0]), (values[1], pools[p][1])])
            before, after = pltpu.roll(mean, 1, 0), pltpu.roll(mean, count - 1, 0)
            mean = jnp.where(group == 0, before, jnp.where(group == 3, after, mean))
            for y in range(SKIP_LINES):
                line = mean[y * 32 : y * 32 + 32]
                west = edge_mean[p, 0, pl.ds(g * SKIP_LINES + y, 1), :]
                east = edge_mean[p, 1, pl.ds(g * SKIP_LINES + y, 1), :]
                line = jnp.where((line_row == 0) & (line_group == 0), west, line)
                line = jnp.where((line_row == 31) & (line_group == 3), east, line)
                pooled[p, pl.ds(base + y * 32, 32), :] = line.astype(BF16)
        return 0

    lax.fori_loop(0, 66 // SKIP_LINES, skip_step, 0)

    def last_step(g, _):
        count = LAST_LINES * 32
        base = pl.multiple_of(g * count, count)
        pairs = []
        for dy in range(3):
            for p in range(2):
                at = (dy * 2 + p) * 256
                pairs.append((pooled[p, pl.ds(base + dy * 32, count), :], wc[at : at + 256, :]))
        coarse = jnp.maximum(add_dots(pairs), 0.0).astype(BF16)
        joined = []
        for side in range(2):
            upward = dot(coarse[:, side * 128 : side * 128 + 128], wu[...])
            upward = upward + skip[side, pl.ds(base + 32, count), :].astype(F32)
            joined.append(jnp.maximum(upward, 0.0).astype(BF16))
        for eight in range(LAST_LINES // 8):
            blocks = [
                joined[side][eight * 256 + half * 128 : eight * 256 + half * 128 + 128] for side in range(2) for half in range(2)
            ]
            logits = dot(jnp.concatenate(blocks, axis=1), wh[...]).T
            top = logits.astype(BF16)
            rest = (logits - top.astype(F32)).astype(BF16)
            for half in range(2):
                rows = pl.ds(pl.multiple_of(g * (LAST_LINES * 4), LAST_LINES * 4) + eight * 32 + half * 16, 16)
                for side in range(2):
                    for px in range(2):
                        at = side * 64 + half * 32 + px * 16
                        lanes = slice((side * 2 + px) * 128, (side * 2 + px) * 128 + 128)
                        high[rows, lanes] = top[at : at + 16]
                        low[rows, lanes] = rest[at : at + 16]
        return 0

    lax.fori_loop(0, 64 // LAST_LINES, last_step, 0)

    at, to = iota((128, 512), 0), iota((128, 512), 1)
    same_line = at // 32 == to // 128
    offset = to % 128 - 4 * (at % 32)
    place = jnp.concatenate(
        [jnp.where(same_line & (offset == part), 1.0, 0.0).astype(BF16) for part in range(4)], axis=0
    )
    logits = dot(high[...], place) + dot(low[...], place)
    for line in range(4):
        mixed[line] = logits[:, line * 128 : line * 128 + 128]
    for k in range(3):
        for z in range(2):
            for py in range(2):
                for line in range(4):
                    row = k * 4 + z * 2 + py
                    out[0, k, z, pl.ds(2 * line + py, 16, stride=8), :] = mixed[line, pl.ds(row, 16, stride=16), :]


def on_device(em_volume, neighbours, first_kernel, second_kernel, coarse_kernel, up_kernel, head_kernel):
    own = em_volume[0]
    steps = lax.axis_size("gz")
    prev = lax.ppermute(own, "gz", [(i, i + 1) for i in range(steps - 1)])
    nxt = lax.ppermute(own, "gz", [(i + 1, i) for i in range(steps - 1)])
    limit = pltpu.CompilerParams(vmem_limit_bytes=56 * 2**20)

    shapes = [(256, 2304), (2048, 256), (1536, 256), (128, 256), (1024, 128)]
    weights = pl.pallas_call(
        weights_kernel,
        out_shape=[jax.ShapeDtypeStruct(s, BF16) for s in shapes],
        in_specs=[VMEM] * 5,
        out_specs=[VMEM] * 5,
        scratch_shapes=[
            pltpu.VMEM((896, 128), F32),
            pltpu.VMEM((864, 128), F32),
            pltpu.VMEM((128, 128), F32),
            pltpu.VMEM((28, 8, 128), F32),
        ],
        compiler_params=limit,
        cost_estimate=pl.CostEstimate(flops=10**8, bytes_accessed=4 * 10**6, transcendentals=0),
        name="weights",
    )(
        first_kernel.T,
        jnp.transpose(second_kernel, (2, 0, 1)),
        jnp.transpose(coarse_kernel, (2, 1, 0)),
        jnp.transpose(up_kernel, (0, 2, 1)),
        head_kernel,
    )

    slots = pl.pallas_call(
        pack_kernel,
        out_shape=jax.ShapeDtypeStruct((32, 24, 128), BF16),
        in_specs=[SMEM] + [VMEM] * 3,
        out_specs=VMEM,
        scratch_shapes=[pltpu.VMEM((4, 24, 128), F32)],
        compiler_params=limit,
        name="pack",
    )(neighbours, prev, own, nxt)
    recv = lax.all_to_all(slots, "xy", 0, 0, tiled=True)

    place = jnp.full((1, 1), lax.axis_index("gz"), jnp.int32)
    meta = jnp.concatenate([neighbours, place], axis=1)
    return pl.pallas_call(
        main_kernel,
        out_shape=jax.ShapeDtypeStruct((1, 3, 2, 128, 128), F32),
        in_specs=[SMEM] + [VMEM] * 9,
        out_specs=VMEM,
        scratch_shapes=[
            pltpu.VMEM((8, 144, 128), F32),
            pltpu.VMEM((8, 40, 128), F32),
            pltpu.VMEM((9, 144, 128), F32),
            pltpu.VMEM((68 * 32, 128), BF16),
            pltpu.VMEM((2, 88, 128), F32),
            pltpu.VMEM((67 * 32, 2304), BF16),
            pltpu.VMEM((2, 2, 80, 256), F32),
            pltpu.VMEM((2, LINES * 32, 256), BF16),
            pltpu.VMEM((2, LINES * 32, 256), BF16),
            pltpu.VMEM((256, 512), BF16),
            pltpu.VMEM((256, 512), BF16),
            pltpu.VMEM((4, 256, 128), F32),
        ],
        compiler_params=limit,
        name="layers",
    )(meta, prev, own, nxt, recv, *weights)


def solution(mesh):
    placed = (P("xy", "gz", None, None), P("xy", None), P(), P(), P(), P(), P())
    return jax.shard_map(
        on_device,
        mesh=mesh,
        in_specs=placed,
        out_specs=P("xy", None, "gz", None, None),
        check_vma=False,
    )
```

time: 72.9 us -> 55.8 us (0.77)
  Pallas kernels: 46.1 us -> 31.4 us
  local copies, waits for them, and re-layouts: 7.75 us -> 1.31 us
  waiting for transfers between devices: 1.61 us -> 5.79 us
    pallas_call x1, Pallas kernels: 40.8 us -> 26.1 us  [on_device(): pl.pallas_call(main_kernel, out_shape=jax.ShapeDtypeStruct((1, 3, 2, 128,...]
    all_to_all x1, waiting for transfers between devices: 0.01 us -> 4.18 us  [on_device(): recv = lax.all_to_all(slots, 'xy', 0, 0, tiled=True)]
    unnamed x15 -> x8, local copies, waits for them, and re-layouts: 4.01 us -> 1.31 us
    pad x3 -> x0, local copies, waits for them, and re-layouts: 1.88 us -> none  [the longest x1 0.65 us: on_device(): coarse = jnp.pad(coarse_kernel.reshape(56, 756), ((0, 8), (0, 12)))]
    reshape x4 -> x0, local copies, waits for them, and re-layouts: 1.86 us -> none  [the longest x2 1.49 us: on_device(): coarse = jnp.pad(coarse_kernel.reshape(56, 756), ((0, 8), (0, 12)))]
  transfers between devices with their start and end apart: 3 -> 3, of which waited for: 1 -> 2; matrix products, arithmetic and copies ran while one was open for 10% -> 1% of each run, Pallas kernels for 5% -> 6%
where the time goes in v2:
time: 55.8 us; the launch traced here: 55.3 us
  Pallas kernels  31.4 us (56%)
  starting transfers between devices  16.1 us (29%)
  waiting for transfers between devices  5.79 us (10%)
  local copies, waits for them, and re-layouts  1.31 us (2%)
  other arithmetic  0.59 us (1%)
    pallas_call x1, Pallas kernels, on_device(): pl.pallas_call(main_kernel, out_shape=jax.ShapeDtypeStruct((1, 3, 2, 128,...  26.1 us
    all_to_all x1, starting transfers between devices, on_device(): recv = lax.all_to_all(slots, 'xy', 0, 0, tiled=True)  10.1 us
    ppermute x1, starting transfers between devices, on_device(): prev = lax.ppermute(own, 'gz', [(i, i + 1) for i in range(steps - 1)])  4.58 us
    all_to_all x1, waiting for transfers between devices, on_device(): recv = lax.all_to_all(slots, 'xy', 0, 0, tiled=True)  4.18 us
    pallas_call x1, Pallas kernels, on_device(): pl.pallas_call(weights_kernel, out_shape=[jax.ShapeDtypeStruct(s, BF16) f...  3.55 us
    pallas_call x1, Pallas kernels, on_device(): pl.pallas_call(pack_kernel, out_shape=jax.ShapeDtypeStruct((32, 24, 128),...  1.78 us
    ppermute x1, waiting for transfers between devices, on_device(): prev = lax.ppermute(own, 'gz', [(i, i + 1) for i in range(steps - 1)])  1.61 us
    ppermute x1, starting transfers between devices, on_device(): nxt = lax.ppermute(own, 'gz', [(i + 1, i) for i in range(steps - 1)])  1.41 us
  transfers between devices with their start and end apart: 3, of which 2 were waited for; matrix products, arithmetic and copies ran while one was open for 1% of the time, Pallas kernels for 6%

profile of v2, /device:TPU:1, one launch (start us, length us, event | category | flops | bytes accessed | tf_op | source)
XLA Modules:
  0.0 55.3 jit_solution(9265860541886763971)
XLA Ops:
  0.0 0.0 copy-start.3
  0.0 1.4 %collective-permute-start.1 = (bf16[2,128,128]{2,1,0:T(8,128)(2,1)}, bf16[2,128,128]{2,1,0:T(8,128)(2,1)S(1)}, u32[]{:S(2)}, u32[]{:S(2)}) collective-permute-start(bf16[2,128,128]{2,1,0:T(8,128)(2,1)} %bitcast.6), channel_id=1, source_target_pairs={{32,0},{64,32},{96,64},{33,1},{65,33},{97,65},{34,2},{66,34},{98,6... | collective-permute-start | bytes 196616 | tf_op jit(solution)/shard_map/ppermute | solution.py:313
  1.4 4.6 %collective-permute-start = (bf16[2,128,128]{2,1,0:T(8,128)(2,1)}, bf16[2,128,128]{2,1,0:T(8,128)(2,1)S(1)}, u32[]{:S(2)}, u32[]{:S(2)}) collective-permute-start(bf16[2,128,128]{2,1,0:T(8,128)(2,1)} %bitcast.7), channel_id=1, source_target_pairs={{0,32},{32,64},{64,96},{1,33},{33,65},{65,97},{2,34},{34,66},{66,9... | collective-permute-start | bytes 196616 | tf_op jit(solution)/shard_map/ppermute | solution.py:312
  6.0 0.0 collective-permute-done.1.nxt
  6.0 0.0 copy-start.1
  6.0 1.6 %collective-permute-done.prev = bf16[2,128,128]{2,1,0:T(8,128)(2,1)S(1)} collective-permute-done((bf16[2,128,128]{2,1,0:T(8,128)(2,1)}, bf16[2,128,128]{2,1,0:T(8,128)(2,1)S(1)}, u32[]{:S(2)}, u32[]{:S(2)}) %collective-permute-start) | collective-permute-done | bytes 65568 | tf_op jit(solution)/shard_map/ppermute | solution.py:312
  7.6 0.0 copy-done.1
  7.6 0.0 copy-start.2
  7.6 0.6 %copy-done.2 = bf16[2,128,128]{2,1,0:T(8,128)(2,1)} copy-done((bf16[2,128,128]{2,1,0:T(8,128)(2,1)}, bf16[2,128,128]{2,1,0:T(8,128)(2,1)S(1)}, u32[]{:S(2)}) %copy-start.2) | copy-done | bytes 65560
  8.3 1.8 %pack.1 = bf16[32,24,128]{2,1,0:T(8,128)(2,1)} custom-call(s32[1,8]{1,0:T(1,128)} %nb.1, bf16[2,128,128]{2,1,0:T(8,128)(2,1)} %copy-done.2, bf16[2,128,128]{2,1,0:T(8,128)(2,1)} %bitcast.8, bf16[2,128,128]{2,1,0:T(8,128)(2,1)} %copy-done.1), custom_call_target="tpu_custom_call" | custom-call | tf_op jit(solution)/shard_map/pack/pallas_call | solution.py:339
  10.0 10.1 %all-to-all-start = ((bf16[32,24,128]{2,1,0:T(8,128)(2,1)}), bf16[32,24,128]{2,1,0:T(8,128)(2,1)S(1)}, u32[]{:S(2)}, u32[]{:S(2)}) async-start(bf16[32,24,128]{2,1,0:T(8,128)(2,1)} %pack.1), calls=%async_computation | async-start | bytes 393216 | tf_op jit(solution)/shard_map/all_to_all | solution.py:348
  20.2 3.6 %weights.1 = (bf16[256,2304]{1,0:T(8,128)(2,1)}, bf16[2048,256]{1,0:T(8,128)(2,1)}, bf16[1536,256]{1,0:T(8,128)(2,1)}, bf16[128,256]{1,0:T(8,128)(2,1)}, bf16[1024,128]{1,0:T(8,128)(2,1)}) custom-call(bf16[9,28]{1,0:T(8,128)(2,1)} %bitcast.13, bf16[27,28,28]{2,1,0:T(8,128)(2,1)} %bitcast.10, bf16[27,28,56]{2,1,0:T(8,128)(2,1)} %bitcast.11, ...), custom_call_target="tpu_custom_call" | custom-call | flops 100000000 | bytes 4000000 | tf_op jit(solution)/shard_map/weights/pallas_call | solution.py:317
  23.7 0.0 copy-done.3
  23.8 0.6 %pad_add_fusion.meta = s32[1,9]{1,0:T(1,128)} fusion(s32[1,1]{1,0:T(1,128)} %bitcast, s32[1,8]{1,0:T(1,128)S(1)} %copy-done.3), kind=kLoop, calls=%fused_computation | loop fusion | flops 9 | bytes 72 | tf_op jit(solution)/shard_map/concatenate | solution.py:351
  24.3 4.2 %all-to-all-done.recv = bf16[32,24,128]{2,1,0:T(8,128)(2,1)S(1)} async-done(((bf16[32,24,128]{2,1,0:T(8,128)(2,1)}), bf16[32,24,128]{2,1,0:T(8,128)(2,1)S(1)}, u32[]{:S(2)}, u32[]{:S(2)}) %all-to-all-start) | async-done | bytes 196640 | tf_op jit(solution)/shard_map/all_to_all | solution.py:348
  28.5 0.0 copy-start
  28.5 0.7 %copy-done = bf16[32,24,128]{2,1,0:T(8,128)(2,1)} copy-done((bf16[32,24,128]{2,1,0:T(8,128)(2,1)}, bf16[32,24,128]{2,1,0:T(8,128)(2,1)S(1)}, u32[]{:S(2)}) %copy-start) | copy-done | bytes 196632
  29.2 26.1 %layers.1 = f32[1,3,2,128,128]{4,3,2,1,0:T(8,128)} custom-call(s32[1,9]{1,0:T(1,128)} %pad_add_fusion.meta, bf16[2,128,128]{2,1,0:T(8,128)(2,1)} %copy-done.2, bf16[2,128,128]{2,1,0:T(8,128)(2,1)} %bitcast.9, bf16[2,128,128]{2,1,0:T(8,128)(2,1)} %copy-done.1, bf16[32,24,128]{2,1,0:T(8,128)(2,1)} %copy-done, bf16[256,2304]{1,0:T(8,128)(2,1)} %get-tuple-element.10.wf, ...), custom_call_target="tpu_custom_call" | custom-call | tf_op jit(solution)/shard_map/layers/pallas_call | solution.py:352
Async XLA Ops:
  0.0 23.7 %copy-start.3 = (s32[1,8]{1,0:T(1,128)S(1)}, s32[1,8]{1,0:T(1,128)}, u32[]{:S(2)}) copy-start(s32[1,8]{1,0:T(1,128)} %nb.1) | copy-start | bytes 100
  0.0 6.0 %collective-permute-start.1 = (bf16[2,128,128]{2,1,0:T(8,128)(2,1)}, bf16[2,128,128]{2,1,0:T(8,128)(2,1)S(1)}, u32[]{:S(2)}, u32[]{:S(2)}) collective-permute-start(bf16[2,128,128]{2,1,0:T(8,128)(2,1)} %bitcast.6), channel_id=1, source_target_pairs={{32,0},{64,32},{96,64},{33,1},{65,33},{97,65},{34,2},{66,34},{98,6... | collective-permute-start | bytes 196616 | tf_op jit(solution)/shard_map/ppermute | solution.py:313
  1.4 6.2 %collective-permute-start = (bf16[2,128,128]{2,1,0:T(8,128)(2,1)}, bf16[2,128,128]{2,1,0:T(8,128)(2,1)S(1)}, u32[]{:S(2)}, u32[]{:S(2)}) collective-permute-start(bf16[2,128,128]{2,1,0:T(8,128)(2,1)} %bitcast.7), channel_id=1, source_target_pairs={{0,32},{32,64},{64,96},{1,33},{33,65},{65,97},{2,34},{34,66},{66,9... | collective-permute-start | bytes 196616 | tf_op jit(solution)/shard_map/ppermute | solution.py:312
  6.0 1.6 %copy-start.1 = (bf16[2,128,128]{2,1,0:T(8,128)(2,1)}, bf16[2,128,128]{2,1,0:T(8,128)(2,1)S(1)}, u32[]{:S(2)}) copy-start(bf16[2,128,128]{2,1,0:T(8,128)(2,1)S(1)} %collective-permute-done.1.nxt) | copy-start | bytes 196612
  7.6 0.6 %copy-start.2 = (bf16[2,128,128]{2,1,0:T(8,128)(2,1)}, bf16[2,128,128]{2,1,0:T(8,128)(2,1)S(1)}, u32[]{:S(2)}) copy-start(bf16[2,128,128]{2,1,0:T(8,128)(2,1)S(1)} %collective-permute-done.prev) | copy-start | bytes 196612
  10.0 18.5 %all-to-all-start = ((bf16[32,24,128]{2,1,0:T(8,128)(2,1)}), bf16[32,24,128]{2,1,0:T(8,128)(2,1)S(1)}, u32[]{:S(2)}, u32[]{:S(2)}) async-start(bf16[32,24,128]{2,1,0:T(8,128)(2,1)} %pack.1), calls=%async_computation | async-start | bytes 393216 | tf_op jit(solution)/shard_map/all_to_all | solution.py:348
  28.5 0.7 %copy-start = (bf16[32,24,128]{2,1,0:T(8,128)(2,1)}, bf16[32,24,128]{2,1,0:T(8,128)(2,1)S(1)}, u32[]{:S(2)}) copy-start(bf16[32,24,128]{2,1,0:T(8,128)(2,1)S(1)} %all-to-all-done.recv) | copy-start | bytes 589828

commit v3 on v2

--- a/solution.py
+++ b/solution.py
@@ -8,7 +8,7 @@
 F32 = jnp.float32
 BF16 = jnp.bfloat16
 LINES = 66
-FIRST_LINES, SKIP_LINES, LAST_LINES = 22, 22, 32
+FIRST_LINES, SKIP_LINES, LAST_LINES, LAST_PART = 66, 33, 32, 32
 FIRST_OFF = 256.0
 SKIP_OFF = 65536.0
 VMEM = pl.BlockSpec(memory_space=pltpu.VMEM)
@@ -28,26 +28,28 @@
     return lax.dot_general(a, b, NT, preferred_element_type=F32)
 
 
-def pack_kernel(nb, prev, own, nxt, slots, rows):
-    slots[...] = jnp.zeros(slots.shape, BF16)
+def pack_kernel(nb, place, own, slots, sent, rows):
+    sent[...] = own[...]
     lane, line = iota((16, 128), 1), iota((16, 128), 0)
     edge = jnp.where((lane == jnp.where(line < 4, line, 120 + line)) & (line < 8), 1.0, 0.0).astype(BF16)
-    planes = jnp.concatenate([ref[z] for ref in (prev, own, nxt) for z in range(2)], axis=0)
+    planes = jnp.concatenate([own[0], own[1]], axis=0)
     sides = dot_nt(edge, planes)
-    for z in range(6):
+    for z in range(2):
         at = slice(4 * z, 4 * z + 4)
         rows[0, at, :] = planes[z * 128 : z * 128 + 16].astype(F32)[0:4]
         rows[1, at, :] = planes[z * 128 + 112 : z * 128 + 128].astype(F32)[12:16]
         rows[2, at, :] = sides[0:4, z * 128 : z * 128 + 128]
         rows[3, at, :] = sides[4:8, z * 128 : z * 128 + 128]
-    for k, strip in enumerate((0, 1, 2, 3, 2, 3, 2, 3)):
-
-        @pl.when(nb[0, k] >= 0)
-        def _():
-            slots[jnp.maximum(nb[0, k], 0)] = rows[strip].astype(BF16)
-
-
-def weights_kernel(first, second, coarse, up, head, wf, ws, wc, wu, wh, taps2, tapsc, part, ups):
+    for step in (-1, 0, 1):
+        depth = place[0, 0] + step
+        for k, strip in enumerate((0, 1, 2, 3, 2, 3, 2, 3)):
+
+            @pl.when((nb[0, k] >= 0) & (depth >= 0) & (depth < 4))
+            def _():
+                slots[jnp.clip(depth, 0, 3) * 32 + jnp.maximum(nb[0, k], 0)] = rows[strip].astype(BF16)
+
+
+def weights_kernel(own, first, second, coarse, up, head, wf, ws, wc, wu, wh, taps2, tapsc, part, ups):
     lane = iota((32, 128), 1)
     part[...] = jnp.zeros(part.shape, F32)
     for four in range(7):
@@ -130,22 +132,31 @@
         wh[block * 256 : block * 256 + 256, :] = jnp.where(to // 32 == block, value, 0.0).astype(BF16)
 
 
-def main_kernel(meta, prev, own, nxt, recv, wf, ws, wc, wu, wh, out, ext, strips, turned, taps, edge_taps, first, edge_mean, pooled, skip, high, low, mixed):
+def main_kernel(
+    nb, depth, prev, own, nxt, recv, wf, ws, wc, wu, wh, out, ext, strips, turned, taps,
+    edge_taps, first, edge_mean, pooled, skip, high, low, mixed
+):
+
     strips[...] = jnp.zeros(strips.shape, F32)
+    ext[...] = jnp.zeros(ext.shape, F32)
+    edge_taps[...] = jnp.zeros(edge_taps.shape, F32)
     for k in range(8):
-        have = meta[0, k] >= 0
-        strips[k, 4:28, :] = jnp.where(have, recv[jnp.maximum(meta[0, k], 0)].astype(F32), 0.0)
+        have = nb[0, k] >= 0
+        for step in range(3):
+            near = depth[0, 0] + step - 1
+            strip = recv[jnp.clip(near, 0, 3) * 32 + jnp.maximum(nb[0, k], 0)].astype(F32)
+            strips[k, 4 + 8 * step : 12 + 8 * step, :] = jnp.where(have & (near >= 0) & (near < 4), strip, 0.0)
         strips[k, 28:32, :] = jnp.full((4, 128), jnp.where(have, 0.0, 1.0), F32)
 
-    ext[...] = jnp.zeros(ext.shape, F32)
     for z in range(7):
         if z < 6:
-            ext[z, 4:132, :] = (prev, own, nxt)[z // 2][z % 2].astype(F32)
+            plane = (prev, own, nxt)[z // 2][z % 2].astype(F32)
+            there = (depth[0, 0] > 0, True, depth[0, 0] < 3)[z // 2]
+            ext[z, 4:132, :] = jnp.where(there, plane, 0.0)
         ext[z, 0:4, :] = strips[0, 4 * z + 4 : 4 * z + 8, :]
         ext[z, 132:136, :] = strips[1, 4 * z + 4 : 4 * z + 8, :]
 
     lane = iota((8, 128), 1)
-    edge_taps[...] = jnp.zeros(edge_taps.shape, F32)
     for b in range(9):
         lines = [ext[z, 16 * b : 16 * b + 16, :] for z in range(8)]
         turned[b, 8:136, :] = jnp.concatenate(lines, axis=0).T
@@ -183,9 +194,11 @@
 
     at, to = iota((256, 256), 0), iota((256, 256), 1)
     meets = (at // 128 == to // 128) & (at % 32 == to % 32)
-    outside = ((meta[0, 8] == 0, False), (False, meta[0, 8] == 3))
-    pools = []
+    outside = ((depth[0, 0] == 0, False), (False, depth[0, 0] == 3))
+    pools, scales = [], []
     for p in range(2):
+        low_plane, high_plane = (jnp.where(gone, 0.0, 0.25) for gone in outside[p])
+        scales.append(jnp.where(iota((1, 256), 1) < 128, low_plane, high_plane))
         scale = jnp.where(to < 128, jnp.where(outside[p][0], 0.0, 0.25), jnp.where(outside[p][1], 0.0, 0.25))
         pools.append([jnp.where(meets & ((to // 32) % 2 != par), scale, 0.0).astype(BF16) for par in range(2)])
 
@@ -242,7 +255,15 @@
                 value = jnp.maximum(add_dots(pairs), 0.0).astype(BF16)
                 skip[par, pl.ds(base, count), p * 128 : p * 128 + 128] = value[:, 128 - p * 128 : 256 - p * 128]
                 values.append(value)
-            mean = add_dots([(values[0], pools[p][0]), (values[1], pools[p][1])])
+            sums = []
+            for value in values:
+                value = value.astype(F32)
+                halves = []
+                for half in (value[:, 0:128], value[:, 128:256]):
+                    half = half + pltpu.roll(half, 32, 1)
+                    halves.append(half + pltpu.roll(half, 64, 1))
+                sums.append(jnp.concatenate(halves, axis=1))
+            mean = jnp.where(group % 2 == 1, sums[0], sums[1]) * scales[p]
             before, after = pltpu.roll(mean, 1, 0), pltpu.roll(mean, count - 1, 0)
             mean = jnp.where(group == 0, before, jnp.where(group == 3, after, mean))
             for y in range(SKIP_LINES):
@@ -256,9 +277,9 @@
 
     lax.fori_loop(0, 66 // SKIP_LINES, skip_step, 0)
 
-    def last_step(g, _):
-        count = LAST_LINES * 32
-        base = pl.multiple_of(g * count, count)
+
+    def last_rows(base, top_row):
+        count = LAST_PART * 32
         pairs = []
         for dy in range(3):
             for p in range(2):
@@ -270,21 +291,31 @@
             upward = dot(coarse[:, side * 128 : side * 128 + 128], wu[...])
             upward = upward + skip[side, pl.ds(base + 32, count), :].astype(F32)
             joined.append(jnp.maximum(upward, 0.0).astype(BF16))
-        for eight in range(LAST_LINES // 8):
-            blocks = [
-                joined[side][eight * 256 + half * 128 : eight * 256 + half * 128 + 128] for side in range(2) for half in range(2)
-            ]
-            logits = dot(jnp.concatenate(blocks, axis=1), wh[...]).T
+        eights = range(0, count, 256)
+        blocks = [
+            jnp.concatenate([joined[side][at + half * 128 : at + half * 128 + 128] for at in eights], axis=0)
+            for side in range(2)
+            for half in range(2)
+        ]
+        mapped = dot(jnp.concatenate(blocks, axis=1), wh[...])
+        for eight in range(LAST_PART // 8):
+            logits = mapped[eight * 128 : eight * 128 + 128].T
             top = logits.astype(BF16)
             rest = (logits - top.astype(F32)).astype(BF16)
             for half in range(2):
-                rows = pl.ds(pl.multiple_of(g * (LAST_LINES * 4), LAST_LINES * 4) + eight * 32 + half * 16, 16)
+                rows = pl.ds(top_row + eight * 32 + half * 16, 16)
                 for side in range(2):
                     for px in range(2):
                         at = side * 64 + half * 32 + px * 16
                         lanes = slice((side * 2 + px) * 128, (side * 2 + px) * 128 + 128)
                         high[rows, lanes] = top[at : at + 16]
                         low[rows, lanes] = rest[at : at + 16]
+
+    def last_step(g, _):
+        base = pl.multiple_of(g * (LAST_LINES * 32), LAST_LINES * 32)
+        top_row = pl.multiple_of(g * (LAST_LINES * 4), LAST_LINES * 4)
+        for part in range(LAST_LINES // LAST_PART):
+            last_rows(base + part * LAST_PART * 32, top_row + part * LAST_PART * 4)
         return 0
 
     lax.fori_loop(0, 64 // LAST_LINES, last_step, 0)
@@ -309,15 +340,28 @@
 def on_device(em_volume, neighbours, first_kernel, second_kernel, coarse_kernel, up_kernel, head_kernel):
     own = em_volume[0]
     steps = lax.axis_size("gz")
-    prev = lax.ppermute(own, "gz", [(i, i + 1) for i in range(steps - 1)])
-    nxt = lax.ppermute(own, "gz", [(i + 1, i) for i in range(steps - 1)])
+    place = jnp.full((1, 1), lax.axis_index("gz"), jnp.int32)
     limit = pltpu.CompilerParams(vmem_limit_bytes=56 * 2**20)
+    image = jax.ShapeDtypeStruct(own.shape, BF16)
+
+    slots, sent = pl.pallas_call(
+        pack_kernel,
+        out_shape=[jax.ShapeDtypeStruct((128, 8, 128), BF16), image],
+        in_specs=[SMEM, SMEM, VMEM],
+        out_specs=[VMEM, VMEM],
+        scratch_shapes=[pltpu.VMEM((4, 8, 128), F32)],
+        compiler_params=limit,
+        name="pack",
+    )(neighbours, place, own)
+    recv = lax.all_to_all(slots, ("gz", "xy"), 0, 0, tiled=True)
+    prev = lax.ppermute(sent, "gz", [(i, (i + 1) % steps) for i in range(steps)])
+    nxt = lax.ppermute(sent, "gz", [((i + 1) % steps, i) for i in range(steps)])
 
     shapes = [(256, 2304), (2048, 256), (1536, 256), (128, 256), (1024, 128)]
     weights = pl.pallas_call(
         weights_kernel,
         out_shape=[jax.ShapeDtypeStruct(s, BF16) for s in shapes],
-        in_specs=[VMEM] * 5,
+        in_specs=[VMEM] * 6,
         out_specs=[VMEM] * 5,
         scratch_shapes=[
             pltpu.VMEM((896, 128), F32),
@@ -329,6 +373,7 @@
         cost_estimate=pl.CostEstimate(flops=10**8, bytes_accessed=4 * 10**6, transcendentals=0),
         name="weights",
     )(
+        sent,
         first_kernel.T,
         jnp.transpose(second_kernel, (2, 0, 1)),
         jnp.transpose(coarse_kernel, (2, 1, 0)),
@@ -336,23 +381,10 @@
         head_kernel,
     )
 
-    slots = pl.pallas_call(
-        pack_kernel,
-        out_shape=jax.ShapeDtypeStruct((32, 24, 128), BF16),
-        in_specs=[SMEM] + [VMEM] * 3,
-        out_specs=VMEM,
-        scratch_shapes=[pltpu.VMEM((4, 24, 128), F32)],
-        compiler_params=limit,
-        name="pack",
-    )(neighbours, prev, own, nxt)
-    recv = lax.all_to_all(slots, "xy", 0, 0, tiled=True)
-
-    place = jnp.full((1, 1), lax.axis_index("gz"), jnp.int32)
-    meta = jnp.concatenate([neighbours, place], axis=1)
     return pl.pallas_call(
         main_kernel,
         out_shape=jax.ShapeDtypeStruct((1, 3, 2, 128, 128), F32),
-        in_specs=[SMEM] + [VMEM] * 9,
+        in_specs=[SMEM] * 2 + [VMEM] * 9,
         out_specs=VMEM,
         scratch_shapes=[
             pltpu.VMEM((8, 144, 128), F32),
@@ -370,7 +402,7 @@
         ],
         compiler_params=limit,
         name="layers",
-    )(meta, prev, own, nxt, recv, *weights)
+    )(neighbours, place, prev, own, nxt, recv, *weights)
 
 
 def solution(mesh):

time: 55.8 us -> 49.6 us (0.89)
  starting transfers between devices: 16.1 us -> 14.2 us
  Pallas kernels: 31.4 us -> 29.8 us
  waiting for transfers between devices: 5.79 us -> 4.68 us
  local copies, waits for them, and re-layouts: 1.31 us -> 0.71 us
  other arithmetic: 0.59 us -> 0 us
    ppermute x2, starting transfers between devices: 5.99 us -> 2.67 us  [the longest x1 2.67 us: on_device(): nxt = lax.ppermute(sent, 'gz', [((i + 1) % steps, i) for i in range(steps)])]
    pallas_call x1, Pallas kernels: 26.1 us -> 24.4 us  [on_device(): pl.pallas_call(main_kernel, out_shape=jax.ShapeDtypeStruct((1, 3, 2, 128,...]
    all_to_all x1, starting transfers between devices: 10.1 us -> 11.5 us  [on_device(): recv = lax.all_to_all(slots, ('gz', 'xy'), 0, 0, tiled=True)]
    all_to_all x1, waiting for transfers between devices: 4.18 us -> 3.42 us  [on_device(): recv = lax.all_to_all(slots, ('gz', 'xy'), 0, 0, tiled=True)]
    unnamed x8 -> x6, local copies, waits for them, and re-layouts: 1.31 us -> 0.71 us
    concatenate x1 -> x0, other arithmetic: 0.59 us -> none  [on_device(): meta = jnp.concatenate([neighbours, place], axis=1)]
  transfers between devices with their start and end apart: 3 -> 3, of which waited for: 2 -> 2; matrix products, arithmetic and copies ran while one was open for 1% -> 0% of each run, Pallas kernels for 6% -> 7%
where the time goes in v3:
time: 49.6 us; the launch traced here: 49.4 us
  Pallas kernels  29.8 us (60%)
  starting transfers between devices  14.2 us (29%)
  waiting for transfers between devices  4.68 us (9%)
  local copies, waits for them, and re-layouts  0.71 us (1%)
    pallas_call x1, Pallas kernels, on_device(): pl.pallas_call(main_kernel, out_shape=jax.ShapeDtypeStruct((1, 3, 2, 128,...  24.4 us
    all_to_all x1, starting transfers between devices, on_device(): recv = lax.all_to_all(slots, ('gz', 'xy'), 0, 0, tiled=True)  11.5 us
    pallas_call x1, Pallas kernels, on_device(): pl.pallas_call(weights_kernel, out_shape=[jax.ShapeDtypeStruct(s, BF16) f...  3.57 us
    all_to_all x1, waiting for transfers between devices, on_device(): recv = lax.all_to_all(slots, ('gz', 'xy'), 0, 0, tiled=True)  3.42 us
    ppermute x1, starting transfers between devices, on_device(): nxt = lax.ppermute(sent, 'gz', [((i + 1) % steps, i) for i in range(steps)])  2.67 us
    pallas_call x1, Pallas kernels, on_device(): pl.pallas_call(pack_kernel, out_shape=[jax.ShapeDtypeStruct((128, 8, 128)...  1.87 us
    ppermute x1, waiting for transfers between devices, on_device(): lax.ppermute(sent, 'gz', [(i, (i + 1) % steps) for i in range(steps)])  1.25 us
  transfers between devices with their start and end apart: 3, of which 2 were waited for; matrix products, arithmetic and copies ran while one was open for 0% of the time, Pallas kernels for 7%

profile of v3, /device:TPU:1, one launch (start us, length us, event | category | flops | bytes accessed | tf_op | source)
XLA Modules:
  0.0 49.4 jit_solution(15523925212642396887)
XLA Ops:
  0.0 1.9 %pack.1 = (bf16[128,8,128]{2,1,0:T(8,128)(2,1)}, bf16[2,128,128]{2,1,0:T(8,128)(2,1)}) custom-call(s32[1,8]{1,0:T(1,128)} %nb.3, s32[1,1]{1,0:T(1,128)} %bitcast.place.depth, bf16[2,128,128]{2,1,0:T(8,128)(2,1)} %bitcast.6), custom_call_target="tpu_custom_call" | custom-call | tf_op jit(solution)/shard_map/pack/pallas_call | solution.py:347
  1.9 11.5 %all-to-all-start = ((bf16[128,8,128]{2,1,0:T(8,128)(2,1)}), bf16[128,8,128]{2,1,0:T(8,128)(2,1)S(1)}, u32[]{:S(2)}, u32[]{:S(2)}) async-start(bf16[128,8,128]{2,1,0:T(8,128)(2,1)} %get-tuple-element.13), calls=%async_computation | async-start | bytes 524288 | tf_op jit(solution)/shard_map/all_to_all | solution.py:356
  13.4 2.7 %collective-permute-start.1 = (bf16[2,128,128]{2,1,0:T(8,128)(2,1)}, bf16[2,128,128]{2,1,0:T(8,128)(2,1)S(1)}, u32[]{:S(2)}, u32[]{:S(2)}) collective-permute-start(bf16[2,128,128]{2,1,0:T(8,128)(2,1)} %get-tuple-element.12.own), channel_id=1, source_target_pairs={{32,0},{64,32},{96,64},{0,96},{33,1},{65,33},{97,65},{1,97},{34,2}... | collective-permute-start | bytes 196616 | tf_op jit(solution)/shard_map/ppermute | solution.py:358
  16.0 0.0 collective-permute-start
  16.0 3.6 %weights.1 = (bf16[256,2304]{1,0:T(8,128)(2,1)}, bf16[2048,256]{1,0:T(8,128)(2,1)}, bf16[1536,256]{1,0:T(8,128)(2,1)}, bf16[128,256]{1,0:T(8,128)(2,1)}, bf16[1024,128]{1,0:T(8,128)(2,1)}) custom-call(bf16[2,128,128]{2,1,0:T(8,128)(2,1)} %get-tuple-element.12.own, bf16[9,28]{1,0:T(8,128)(2,1)} %bitcast.11, bf16[27,28,28]{2,1,0:T(8,128)(2,1)} %bitcast.8, ...), custom_call_target="tpu_custom_call" | custom-call | flops 100000000 | bytes 4000000 | tf_op jit(solution)/shard_map/weights/pallas_call | solution.py:361
  19.6 0.0 collective-permute-done.1.nxt
  19.6 0.0 copy-start.1
  19.6 1.3 %collective-permute-done.prev = bf16[2,128,128]{2,1,0:T(8,128)(2,1)S(1)} collective-permute-done((bf16[2,128,128]{2,1,0:T(8,128)(2,1)}, bf16[2,128,128]{2,1,0:T(8,128)(2,1)S(1)}, u32[]{:S(2)}, u32[]{:S(2)}) %collective-permute-start) | collective-permute-done | bytes 65568 | tf_op jit(solution)/shard_map/ppermute | solution.py:357
  20.9 0.0 copy-start.2
  20.9 3.4 %all-to-all-done.recv = bf16[128,8,128]{2,1,0:T(8,128)(2,1)S(1)} async-done(((bf16[128,8,128]{2,1,0:T(8,128)(2,1)}), bf16[128,8,128]{2,1,0:T(8,128)(2,1)S(1)}, u32[]{:S(2)}, u32[]{:S(2)}) %all-to-all-start) | async-done | bytes 262176 | tf_op jit(solution)/shard_map/all_to_all | solution.py:356
  24.3 0.0 copy-start
  24.3 0.0 copy-done.1
  24.3 0.0 copy-done.2
  24.3 0.7 %copy-done = bf16[128,8,128]{2,1,0:T(8,128)(2,1)} copy-done((bf16[128,8,128]{2,1,0:T(8,128)(2,1)}, bf16[128,8,128]{2,1,0:T(8,128)(2,1)S(1)}, u32[]{:S(2)}) %copy-start) | copy-done | bytes 262168
  25.0 24.4 %layers.1 = f32[1,3,2,128,128]{4,3,2,1,0:T(8,128)} custom-call(s32[1,8]{1,0:T(1,128)} %nb.3, s32[1,1]{1,0:T(1,128)} %bitcast.place.depth, bf16[2,128,128]{2,1,0:T(8,128)(2,1)} %copy-done.2, bf16[2,128,128]{2,1,0:T(8,128)(2,1)} %bitcast.7, bf16[2,128,128]{2,1,0:T(8,128)(2,1)} %copy-done.1, bf16[128,8,128]{2,1,0:T(8,128)(2,1)} %copy-done, ...), custom_call_target="tpu_custom_call" | custom-call | tf_op jit(solution)/shard_map/layers/pallas_call | solution.py:384
Async XLA Ops:
  1.9 22.4 %all-to-all-start = ((bf16[128,8,128]{2,1,0:T(8,128)(2,1)}), bf16[128,8,128]{2,1,0:T(8,128)(2,1)S(1)}, u32[]{:S(2)}, u32[]{:S(2)}) async-start(bf16[128,8,128]{2,1,0:T(8,128)(2,1)} %get-tuple-element.13), calls=%async_computation | async-start | bytes 524288 | tf_op jit(solution)/shard_map/all_to_all | solution.py:356
  13.4 6.2 %collective-permute-start.1 = (bf16[2,128,128]{2,1,0:T(8,128)(2,1)}, bf16[2,128,128]{2,1,0:T(8,128)(2,1)S(1)}, u32[]{:S(2)}, u32[]{:S(2)}) collective-permute-start(bf16[2,128,128]{2,1,0:T(8,128)(2,1)} %get-tuple-element.12.own), channel_id=1, source_target_pairs={{32,0},{64,32},{96,64},{0,96},{33,1},{65,33},{97,65},{1,97},{34,2}... | collective-permute-start | bytes 196616 | tf_op jit(solution)/shard_map/ppermute | solution.py:358
  16.0 4.8 %collective-permute-start = (bf16[2,128,128]{2,1,0:T(8,128)(2,1)}, bf16[2,128,128]{2,1,0:T(8,128)(2,1)S(1)}, u32[]{:S(2)}, u32[]{:S(2)}) collective-permute-start(bf16[2,128,128]{2,1,0:T(8,128)(2,1)} %get-tuple-element.12.own), channel_id=1, source_target_pairs={{0,32},{32,64},{64,96},{96,0},{1,33},{33,65},{65,97},{97,1},{2,34}... | collective-permute-start | bytes 196616 | tf_op jit(solution)/shard_map/ppermute | solution.py:357
  19.6 4.7 %copy-start.1 = (bf16[2,128,128]{2,1,0:T(8,128)(2,1)}, bf16[2,128,128]{2,1,0:T(8,128)(2,1)S(1)}, u32[]{:S(2)}) copy-start(bf16[2,128,128]{2,1,0:T(8,128)(2,1)S(1)} %collective-permute-done.1.nxt) | copy-start | bytes 196612
  20.9 3.4 %copy-start.2 = (bf16[2,128,128]{2,1,0:T(8,128)(2,1)}, bf16[2,128,128]{2,1,0:T(8,128)(2,1)S(1)}, u32[]{:S(2)}) copy-start(bf16[2,128,128]{2,1,0:T(8,128)(2,1)S(1)} %collective-permute-done.prev) | copy-start | bytes 196612
  24.3 0.7 %copy-start = (bf16[128,8,128]{2,1,0:T(8,128)(2,1)}, bf16[128,8,128]{2,1,0:T(8,128)(2,1)S(1)}, u32[]{:S(2)}) copy-start(bf16[128,8,128]{2,1,0:T(8,128)(2,1)S(1)} %all-to-all-done.recv) | copy-start | bytes 786436

commit v4 on v3

--- a/solution.py
+++ b/solution.py
@@ -8,7 +8,9 @@
 F32 = jnp.float32
 BF16 = jnp.bfloat16
 LINES = 66
-FIRST_LINES, SKIP_LINES, LAST_LINES, LAST_PART = 66, 33, 32, 32
+FIRST_AFTER = (1, 3, 5, 8)
+SKIP_STEPS = (22, 22, 22)
+LAST_STEPS = (32, 32)
 FIRST_OFF = 256.0
 SKIP_OFF = 65536.0
 VMEM = pl.BlockSpec(memory_space=pltpu.VMEM)
@@ -157,6 +159,12 @@
         ext[z, 132:136, :] = strips[1, 4 * z + 4 : 4 * z + 8, :]
 
     lane = iota((8, 128), 1)
+    def first_rows(base, count):
+        window = jnp.concatenate([taps[pl.ds(base, count), :], taps[pl.ds(base + 32, count), :]], axis=1)
+        for n in range(0, 2304, 256):
+            first[pl.ds(base, count), n : n + 256] = jnp.maximum(dot(window, wf[:, n : n + 256]), 0.0).astype(BF16)
+
+    done = 0
     for b in range(9):
         lines = [ext[z, 16 * b : 16 * b + 16, :] for z in range(8)]
         turned[b, 8:136, :] = jnp.concatenate(lines, axis=0).T
@@ -191,6 +199,10 @@
                 taps[at * 32 : at * 32 + 32, :] = parts[y][0:32].astype(BF16)
                 edge_taps[0, at : at + 1, :] = parts[y][32:33]
                 edge_taps[1, at : at + 1, :] = parts[y][33:34]
+        if b in FIRST_AFTER:
+            ready = min(8 * b + 7, 67)
+            first_rows(done * 32, (ready - done) * 32)
+            done = ready
 
     at, to = iota((256, 256), 0), iota((256, 256), 1)
     meets = (at // 128 == to // 128) & (at % 32 == to % 32)
@@ -198,7 +210,7 @@
     pools, scales = [], []
     for p in range(2):
         low_plane, high_plane = (jnp.where(gone, 0.0, 0.25) for gone in outside[p])
-        scales.append(jnp.where(iota((1, 256), 1) < 128, low_plane, high_plane))
+        scales.append((low_plane, high_plane))
         scale = jnp.where(to < 128, jnp.where(outside[p][0], 0.0, 0.25), jnp.where(outside[p][1], 0.0, 0.25))
         pools.append([jnp.where(meets & ((to // 32) % 2 != par), scale, 0.0).astype(BF16) for par in range(2)])
 
@@ -226,23 +238,12 @@
         edge_mean[p, 0] = dot(value[0:80], pools[p][1])
         edge_mean[p, 1] = dot(value[80:160], pools[p][0])
 
-    def first_rows(base, count):
-        window = jnp.concatenate([taps[pl.ds(base, count), :], taps[pl.ds(base + 32, count), :]], axis=1)
-        for n in range(0, 2304, 256):
-            first[pl.ds(base, count), n : n + 256] = jnp.maximum(dot(window, wf[:, n : n + 256]), 0.0).astype(BF16)
-
-    def first_step(g, _):
-        first_rows(pl.multiple_of(g * (FIRST_LINES * 32), FIRST_LINES * 32), FIRST_LINES * 32)
-        return 0
-
-    lax.fori_loop(0, 66 // FIRST_LINES, first_step, 0)
-    first_rows(2112, 32)
-
-    def skip_step(g, _):
-        count = SKIP_LINES * 32
-        base = pl.multiple_of(g * count, count)
-        group = (iota((count, 256), 1) // 32) % 4
-        line_row, line_group = iota((32, 256), 0), (iota((32, 256), 1) // 32) % 4
+    group = iota((1, 128), 1) // 32
+    tile_row, tile_group = iota((8, 256), 0), (iota((8, 256), 1) // 32) % 4
+    at_west, at_east = (tile_row == 0) & (tile_group == 0), (tile_row == 7) & (tile_group == 3)
+
+    def skip_rows(top, lines):
+        base, count = top * 32, lines * 32
         for p in range(2):
             values = []
             for par in range(2):
@@ -255,31 +256,33 @@
                 value = jnp.maximum(add_dots(pairs), 0.0).astype(BF16)
                 skip[par, pl.ds(base, count), p * 128 : p * 128 + 128] = value[:, 128 - p * 128 : 256 - p * 128]
                 values.append(value)
-            sums = []
-            for value in values:
-                value = value.astype(F32)
-                halves = []
-                for half in (value[:, 0:128], value[:, 128:256]):
-                    half = half + pltpu.roll(half, 32, 1)
-                    halves.append(half + pltpu.roll(half, 64, 1))
-                sums.append(jnp.concatenate(halves, axis=1))
-            mean = jnp.where(group % 2 == 1, sums[0], sums[1]) * scales[p]
-            before, after = pltpu.roll(mean, 1, 0), pltpu.roll(mean, count - 1, 0)
-            mean = jnp.where(group == 0, before, jnp.where(group == 3, after, mean))
-            for y in range(SKIP_LINES):
-                line = mean[y * 32 : y * 32 + 32]
-                west = edge_mean[p, 0, pl.ds(g * SKIP_LINES + y, 1), :]
-                east = edge_mean[p, 1, pl.ds(g * SKIP_LINES + y, 1), :]
-                line = jnp.where((line_row == 0) & (line_group == 0), west, line)
-                line = jnp.where((line_row == 31) & (line_group == 3), east, line)
-                pooled[p, pl.ds(base + y * 32, 32), :] = line.astype(BF16)
-        return 0
-
-    lax.fori_loop(0, 66 // SKIP_LINES, skip_step, 0)
-
-
-    def last_rows(base, top_row):
-        count = LAST_PART * 32
+            halves = []
+            for half in range(2):
+                sums = []
+                for value in values:
+                    part = value[:, half * 128 : half * 128 + 128].astype(F32)
+                    part = part + pltpu.roll(part, 32, 1)
+                    sums.append(part + pltpu.roll(part, 64, 1))
+                mean = jnp.where(group % 2 == 1, sums[0], sums[1]) * scales[p][half]
+                before, after = pltpu.roll(mean, 1, 0), pltpu.roll(mean, count - 1, 0)
+                halves.append(jnp.where(group == 0, before, jnp.where(group == 3, after, mean)))
+            mean = jnp.concatenate(halves, axis=1)
+            for y in range(lines):
+                west = edge_mean[p, 0, top + y : top + y + 1, :]
+                east = edge_mean[p, 1, top + y : top + y + 1, :]
+                line = [mean[y * 32 + at : y * 32 + at + 8] for at in range(0, 32, 8)]
+                line[0] = jnp.where(at_west, west, line[0])
+                line[3] = jnp.where(at_east, east, line[3])
+                pooled[p, pl.ds(base + y * 32, 32), :] = jnp.concatenate(line, axis=0).astype(BF16)
+
+    top = 0
+    for lines in SKIP_STEPS:
+        skip_rows(top, lines)
+        top += lines
+
+
+    def last_rows(top, lines):
+        base, count = top * 32, lines * 32
         pairs = []
         for dy in range(3):
             for p in range(2):
@@ -298,27 +301,23 @@
             for half in range(2)
         ]
         mapped = dot(jnp.concatenate(blocks, axis=1), wh[...])
-        for eight in range(LAST_PART // 8):
+        for eight in range(lines // 8):
             logits = mapped[eight * 128 : eight * 128 + 128].T
-            top = logits.astype(BF16)
-            rest = (logits - top.astype(F32)).astype(BF16)
+            rounded = logits.astype(BF16)
+            rest = (logits - rounded.astype(F32)).astype(BF16)
             for half in range(2):
-                rows = pl.ds(top_row + eight * 32 + half * 16, 16)
+                rows = pl.ds(top * 4 + eight * 32 + half * 16, 16)
                 for side in range(2):
                     for px in range(2):
                         at = side * 64 + half * 32 + px * 16
                         lanes = slice((side * 2 + px) * 128, (side * 2 + px) * 128 + 128)
-                        high[rows, lanes] = top[at : at + 16]
+                        high[rows, lanes] = rounded[at : at + 16]
                         low[rows, lanes] = rest[at : at + 16]
 
-    def last_step(g, _):
-        base = pl.multiple_of(g * (LAST_LINES * 32), LAST_LINES * 32)
-        top_row = pl.multiple_of(g * (LAST_LINES * 4), LAST_LINES * 4)
-        for part in range(LAST_LINES // LAST_PART):
-            last_rows(base + part * LAST_PART * 32, top_row + part * LAST_PART * 4)
-        return 0
-
-    lax.fori_loop(0, 64 // LAST_LINES, last_step, 0)
+    top = 0
+    for lines in LAST_STEPS:
+        last_rows(top, lines)
+        top += lines
 
     at, to = iota((128, 512), 0), iota((128, 512), 1)
     same_line = at // 32 == to // 128

time: 49.6 us -> 47.9 us (0.966)
  Pallas kernels: 29.8 us -> 28.1 us
    pallas_call x1, Pallas kernels: 24.4 us -> 22.7 us  [on_device(): pl.pallas_call(main_kernel, out_shape=jax.ShapeDtypeStruct((1, 3, 2, 128,...]
where the time goes in v4:
time: 47.9 us; the launch traced here: 47.7 us
  Pallas kernels  28.1 us (59%)
  starting transfers between devices  14.1 us (29%)
  waiting for transfers between devices  4.68 us (10%)
  local copies, waits for them, and re-layouts  0.71 us (1%)
    pallas_call x1, Pallas kernels, on_device(): pl.pallas_call(main_kernel, out_shape=jax.ShapeDtypeStruct((1, 3, 2, 128,...  22.7 us
    all_to_all x1, starting transfers between devices, on_device(): recv = lax.all_to_all(slots, ('gz', 'xy'), 0, 0, tiled=True)  11.5 us
    pallas_call x1, Pallas kernels, on_device(): pl.pallas_call(weights_kernel, out_shape=[jax.ShapeDtypeStruct(s, BF16) f...  3.57 us
    all_to_all x1, waiting for transfers between devices, on_device(): recv = lax.all_to_all(slots, ('gz', 'xy'), 0, 0, tiled=True)  3.42 us
    ppermute x1, starting transfers between devices, on_device(): nxt = lax.ppermute(sent, 'gz', [((i + 1) % steps, i) for i in range(steps)])  2.67 us
    pallas_call x1, Pallas kernels, on_device(): pl.pallas_call(pack_kernel, out_shape=[jax.ShapeDtypeStruct((128, 8, 128)...  1.85 us
    ppermute x1, waiting for transfers between devices, on_device(): lax.ppermute(sent, 'gz', [(i, (i + 1) % steps) for i in range(steps)])  1.25 us
  transfers between devices with their start and end apart: 3, of which 2 were waited for; matrix products, arithmetic and copies ran while one was open for 0% of the time, Pallas kernels for 7%

profile of v4, /device:TPU:1, one launch (start us, length us, event | category | flops | bytes accessed | tf_op | source)
XLA Modules:
  0.0 47.7 jit_solution(13220366139499103489)
XLA Ops:
  0.0 1.9 %pack.1 = (bf16[128,8,128]{2,1,0:T(8,128)(2,1)}, bf16[2,128,128]{2,1,0:T(8,128)(2,1)}) custom-call(s32[1,8]{1,0:T(1,128)} %nb.3, s32[1,1]{1,0:T(1,128)} %bitcast.place.depth, bf16[2,128,128]{2,1,0:T(8,128)(2,1)} %bitcast.6), custom_call_target="tpu_custom_call" | custom-call | tf_op jit(solution)/shard_map/pack/pallas_call | solution.py:346
  1.9 11.5 %all-to-all-start = ((bf16[128,8,128]{2,1,0:T(8,128)(2,1)}), bf16[128,8,128]{2,1,0:T(8,128)(2,1)S(1)}, u32[]{:S(2)}, u32[]{:S(2)}) async-start(bf16[128,8,128]{2,1,0:T(8,128)(2,1)} %get-tuple-element.13), calls=%async_computation | async-start | bytes 524288 | tf_op jit(solution)/shard_map/all_to_all | solution.py:355
  13.3 2.7 %collective-permute-start.1 = (bf16[2,128,128]{2,1,0:T(8,128)(2,1)}, bf16[2,128,128]{2,1,0:T(8,128)(2,1)S(1)}, u32[]{:S(2)}, u32[]{:S(2)}) collective-permute-start(bf16[2,128,128]{2,1,0:T(8,128)(2,1)} %get-tuple-element.12.own), channel_id=1, source_target_pairs={{32,0},{64,32},{96,64},{0,96},{33,1},{65,33},{97,65},{1,97},{34,2}... | collective-permute-start | bytes 196616 | tf_op jit(solution)/shard_map/ppermute | solution.py:357
  16.0 0.0 collective-permute-start
  16.0 3.6 %weights.1 = (bf16[256,2304]{1,0:T(8,128)(2,1)}, bf16[2048,256]{1,0:T(8,128)(2,1)}, bf16[1536,256]{1,0:T(8,128)(2,1)}, bf16[128,256]{1,0:T(8,128)(2,1)}, bf16[1024,128]{1,0:T(8,128)(2,1)}) custom-call(bf16[2,128,128]{2,1,0:T(8,128)(2,1)} %get-tuple-element.12.own, bf16[9,28]{1,0:T(8,128)(2,1)} %bitcast.11, bf16[27,28,28]{2,1,0:T(8,128)(2,1)} %bitcast.8, ...), custom_call_target="tpu_custom_call" | custom-call | flops 100000000 | bytes 4000000 | tf_op jit(solution)/shard_map/weights/pallas_call | solution.py:360
  19.6 0.0 collective-permute-done.1.nxt
  19.6 0.0 copy-start.1
  19.6 1.3 %collective-permute-done.prev = bf16[2,128,128]{2,1,0:T(8,128)(2,1)S(1)} collective-permute-done((bf16[2,128,128]{2,1,0:T(8,128)(2,1)}, bf16[2,128,128]{2,1,0:T(8,128)(2,1)S(1)}, u32[]{:S(2)}, u32[]{:S(2)}) %collective-permute-start) | collective-permute-done | bytes 65568 | tf_op jit(solution)/shard_map/ppermute | solution.py:356
  20.8 0.0 copy-start.2
  20.8 3.4 %all-to-all-done.recv = bf16[128,8,128]{2,1,0:T(8,128)(2,1)S(1)} async-done(((bf16[128,8,128]{2,1,0:T(8,128)(2,1)}), bf16[128,8,128]{2,1,0:T(8,128)(2,1)S(1)}, u32[]{:S(2)}, u32[]{:S(2)}) %all-to-all-start) | async-done | bytes 262176 | tf_op jit(solution)/shard_map/all_to_all | solution.py:355
  24.3 0.0 copy-start
  24.3 0.0 copy-done.1
  24.3 0.0 copy-done.2
  24.3 0.7 %copy-done = bf16[128,8,128]{2,1,0:T(8,128)(2,1)} copy-done((bf16[128,8,128]{2,1,0:T(8,128)(2,1)}, bf16[128,8,128]{2,1,0:T(8,128)(2,1)S(1)}, u32[]{:S(2)}) %copy-start) | copy-done | bytes 262168
  25.0 22.7 %layers.1 = f32[1,3,2,128,128]{4,3,2,1,0:T(8,128)} custom-call(s32[1,8]{1,0:T(1,128)} %nb.3, s32[1,1]{1,0:T(1,128)} %bitcast.place.depth, bf16[2,128,128]{2,1,0:T(8,128)(2,1)} %copy-done.2, bf16[2,128,128]{2,1,0:T(8,128)(2,1)} %bitcast.7, bf16[2,128,128]{2,1,0:T(8,128)(2,1)} %copy-done.1, bf16[128,8,128]{2,1,0:T(8,128)(2,1)} %copy-done, ...), custom_call_target="tpu_custom_call" | custom-call | tf_op jit(solution)/shard_map/layers/pallas_call | solution.py:383
Async XLA Ops:
  1.9 22.4 %all-to-all-start = ((bf16[128,8,128]{2,1,0:T(8,128)(2,1)}), bf16[128,8,128]{2,1,0:T(8,128)(2,1)S(1)}, u32[]{:S(2)}, u32[]{:S(2)}) async-start(bf16[128,8,128]{2,1,0:T(8,128)(2,1)} %get-tuple-element.13), calls=%async_computation | async-start | bytes 524288 | tf_op jit(solution)/shard_map/all_to_all | solution.py:355
  13.3 6.2 %collective-permute-start.1 = (bf16[2,128,128]{2,1,0:T(8,128)(2,1)}, bf16[2,128,128]{2,1,0:T(8,128)(2,1)S(1)}, u32[]{:S(2)}, u32[]{:S(2)}) collective-permute-start(bf16[2,128,128]{2,1,0:T(8,128)(2,1)} %get-tuple-element.12.own), channel_id=1, source_target_pairs={{32,0},{64,32},{96,64},{0,96},{33,1},{65,33},{97,65},{1,97},{34,2}... | collective-permute-start | bytes 196616 | tf_op jit(solution)/shard_map/ppermute | solution.py:357
  16.0 4.8 %collective-permute-start = (bf16[2,128,128]{2,1,0:T(8,128)(2,1)}, bf16[2,128,128]{2,1,0:T(8,128)(2,1)S(1)}, u32[]{:S(2)}, u32[]{:S(2)}) collective-permute-start(bf16[2,128,128]{2,1,0:T(8,128)(2,1)} %get-tuple-element.12.own), channel_id=1, source_target_pairs={{0,32},{32,64},{64,96},{96,0},{1,33},{33,65},{65,97},{97,1},{2,34}... | collective-permute-start | bytes 196616 | tf_op jit(solution)/shard_map/ppermute | solution.py:356
  19.6 4.7 %copy-start.1 = (bf16[2,128,128]{2,1,0:T(8,128)(2,1)}, bf16[2,128,128]{2,1,0:T(8,128)(2,1)S(1)}, u32[]{:S(2)}) copy-start(bf16[2,128,128]{2,1,0:T(8,128)(2,1)S(1)} %collective-permute-done.1.nxt) | copy-start | bytes 196612
  20.8 3.4 %copy-start.2 = (bf16[2,128,128]{2,1,0:T(8,128)(2,1)}, bf16[2,128,128]{2,1,0:T(8,128)(2,1)S(1)}, u32[]{:S(2)}) copy-start(bf16[2,128,128]{2,1,0:T(8,128)(2,1)S(1)} %collective-permute-done.prev) | copy-start | bytes 196612
  24.3 0.7 %copy-start = (bf16[128,8,128]{2,1,0:T(8,128)(2,1)}, bf16[128,8,128]{2,1,0:T(8,128)(2,1)S(1)}, u32[]{:S(2)}) copy-start(bf16[128,8,128]{2,1,0:T(8,128)(2,1)S(1)} %all-to-all-done.recv) | copy-start | bytes 786436

commit v5 on v4

--- a/solution.py
+++ b/solution.py
@@ -9,8 +9,8 @@
 BF16 = jnp.bfloat16
 LINES = 66
 FIRST_AFTER = (1, 3, 5, 8)
-SKIP_STEPS = (22, 22, 22)
-LAST_STEPS = (32, 32)
+SKIP_STEPS = (11,) * 6
+LAST_STEPS = (((0, 16), 16), ((32, 48), 16))
 FIRST_OFF = 256.0
 SKIP_OFF = 65536.0
 VMEM = pl.BlockSpec(memory_space=pltpu.VMEM)
@@ -245,15 +245,16 @@
     def skip_rows(top, lines):
         base, count = top * 32, lines * 32
         for p in range(2):
-            values = []
+            totals, values = [None, None], []
+            for z in range(4):
+                for dy in range(2):
+                    at = (z * 2 + dy) * 256
+                    for par in range(2):
+                        lanes = (2 * p + z) * 384 + par * 128
+                        term = dot(first[pl.ds(base + dy * 32, count), lanes : lanes + 256], ws[at : at + 256, :])
+                        totals[par] = term if totals[par] is None else totals[par] + term
             for par in range(2):
-                pairs = []
-                for z in range(4):
-                    for dy in range(2):
-                        lanes = (2 * p + z) * 384 + par * 128
-                        at = (z * 2 + dy) * 256
-                        pairs.append((first[pl.ds(base + dy * 32, count), lanes : lanes + 256], ws[at : at + 256, :]))
-                value = jnp.maximum(add_dots(pairs), 0.0).astype(BF16)
+                value = jnp.maximum(totals[par], 0.0).astype(BF16)
                 skip[par, pl.ds(base, count), p * 128 : p * 128 + 128] = value[:, 128 - p * 128 : 256 - p * 128]
                 values.append(value)
             halves = []
@@ -281,43 +282,47 @@
         top += lines
 
 
-    def last_rows(top, lines):
-        base, count = top * 32, lines * 32
-        pairs = []
+    def last_rows(tops, lines):
+        count = lines * 32
+        totals = [None] * len(tops)
         for dy in range(3):
             for p in range(2):
                 at = (dy * 2 + p) * 256
-                pairs.append((pooled[p, pl.ds(base + dy * 32, count), :], wc[at : at + 256, :]))
-        coarse = jnp.maximum(add_dots(pairs), 0.0).astype(BF16)
-        joined = []
+                for i, top in enumerate(tops):
+                    term = dot(pooled[p, pl.ds(top * 32 + dy * 32, count), :], wc[at : at + 256, :])
+                    totals[i] = term if totals[i] is None else totals[i] + term
+        coarse = [jnp.maximum(total, 0.0).astype(BF16) for total in totals]
+        joined = [[] for _ in tops]
         for side in range(2):
-            upward = dot(coarse[:, side * 128 : side * 128 + 128], wu[...])
-            upward = upward + skip[side, pl.ds(base + 32, count), :].astype(F32)
-            joined.append(jnp.maximum(upward, 0.0).astype(BF16))
-        eights = range(0, count, 256)
+            for i, top in enumerate(tops):
+                upward = dot(coarse[i][:, side * 128 : side * 128 + 128], wu[...])
+                upward = upward + skip[side, pl.ds(top * 32 + 32, count), :].astype(F32)
+                joined[i].append(jnp.maximum(upward, 0.0).astype(BF16))
         blocks = [
-            jnp.concatenate([joined[side][at + half * 128 : at + half * 128 + 128] for at in eights], axis=0)
-            for side in range(2)
-            for half in range(2)
+            [
+                jnp.concatenate([part[side][at + half * 128 : at + half * 128 + 128] for at in range(0, count, 256)], axis=0)
+                for side in range(2)
+                for half in range(2)
+            ]
+            for part in joined
         ]
-        mapped = dot(jnp.concatenate(blocks, axis=1), wh[...])
-        for eight in range(lines // 8):
-            logits = mapped[eight * 128 : eight * 128 + 128].T
-            rounded = logits.astype(BF16)
-            rest = (logits - rounded.astype(F32)).astype(BF16)
-            for half in range(2):
-                rows = pl.ds(top * 4 + eight * 32 + half * 16, 16)
-                for side in range(2):
-                    for px in range(2):
-                        at = side * 64 + half * 32 + px * 16
-                        lanes = slice((side * 2 + px) * 128, (side * 2 + px) * 128 + 128)
-                        high[rows, lanes] = rounded[at : at + 16]
-                        low[rows, lanes] = rest[at : at + 16]
-
-    top = 0
-    for lines in LAST_STEPS:
-        last_rows(top, lines)
-        top += lines
+        mapped = [dot(jnp.concatenate(block, axis=1), wh[...]) for block in blocks]
+        for i, top in enumerate(tops):
+            for eight in range(lines // 8):
+                logits = mapped[i][eight * 128 : eight * 128 + 128].T
+                rounded = logits.astype(BF16)
+                rest = (logits - rounded.astype(F32)).astype(BF16)
+                for half in range(2):
+                    rows = pl.ds(top * 4 + eight * 32 + half * 16, 16)
+                    for side in range(2):
+                        for px in range(2):
+                            at = side * 64 + half * 32 + px * 16
+                            lanes = slice((side * 2 + px) * 128, (side * 2 + px) * 128 + 128)
+                            high[rows, lanes] = rounded[at : at + 16]
+                            low[rows, lanes] = rest[at : at + 16]
+
+    for tops, lines in LAST_STEPS:
+        last_rows(tops, lines)
 
     at, to = iota((128, 512), 0), iota((128, 512), 1)
     same_line = at // 32 == to // 128

time: 47.9 us -> 46 us (0.960)
  Pallas kernels: 28.1 us -> 26.2 us
    pallas_call x1, Pallas kernels: 22.7 us -> 20.8 us  [on_device(): pl.pallas_call(main_kernel, out_shape=jax.ShapeDtypeStruct((1, 3, 2, 128,...]
  transfers between devices with their start and end apart: 3 -> 3, of which waited for: 2 -> 2; matrix products, arithmetic and copies ran while one was open for 0% -> 0% of each run, Pallas kernels for 7% -> 8%
where the time goes in v5:
time: 46 us; the launch traced here: 45.8 us
  Pallas kernels  26.2 us (57%)
  starting transfers between devices  14.2 us (31%)
  waiting for transfers between devices  4.68 us (10%)
  local copies, waits for them, and re-layouts  0.71 us (2%)
    pallas_call x1, Pallas kernels, on_device(): pl.pallas_call(main_kernel, out_shape=jax.ShapeDtypeStruct((1, 3, 2, 128,...  20.8 us
    all_to_all x1, starting transfers between devices, on_device(): recv = lax.all_to_all(slots, ('gz', 'xy'), 0, 0, tiled=True)  11.5 us
    pallas_call x1, Pallas kernels, on_device(): pl.pallas_call(weights_kernel, out_shape=[jax.ShapeDtypeStruct(s, BF16) f...  3.57 us
    all_to_all x1, waiting for transfers between devices, on_device(): recv = lax.all_to_all(slots, ('gz', 'xy'), 0, 0, tiled=True)  3.42 us
    ppermute x1, starting transfers between devices, on_device(): nxt = lax.ppermute(sent, 'gz', [((i + 1) % steps, i) for i in range(steps)])  2.67 us
    pallas_call x1, Pallas kernels, on_device(): pl.pallas_call(pack_kernel, out_shape=[jax.ShapeDtypeStruct((128, 8, 128)...  1.86 us
    ppermute x1, waiting for transfers between devices, on_device(): lax.ppermute(sent, 'gz', [(i, (i + 1) % steps) for i in range(steps)])  1.25 us
  transfers between devices with their start and end apart: 3, of which 2 were waited for; matrix products, arithmetic and copies ran while one was open for 0% of the time, Pallas kernels for 8%

profile of v5, /device:TPU:1, one launch (start us, length us, event | category | flops | bytes accessed | tf_op | source)
XLA Modules:
  0.0 45.8 jit_solution(1712519682377194225)
XLA Ops:
  0.0 1.9 %pack.1 = (bf16[128,8,128]{2,1,0:T(8,128)(2,1)}, bf16[2,128,128]{2,1,0:T(8,128)(2,1)}) custom-call(s32[1,8]{1,0:T(1,128)} %nb.3, s32[1,1]{1,0:T(1,128)} %bitcast.place.depth, bf16[2,128,128]{2,1,0:T(8,128)(2,1)} %bitcast.6), custom_call_target="tpu_custom_call" | custom-call | tf_op jit(solution)/shard_map/pack/pallas_call | solution.py:351
  1.9 11.5 %all-to-all-start = ((bf16[128,8,128]{2,1,0:T(8,128)(2,1)}), bf16[128,8,128]{2,1,0:T(8,128)(2,1)S(1)}, u32[]{:S(2)}, u32[]{:S(2)}) async-start(bf16[128,8,128]{2,1,0:T(8,128)(2,1)} %get-tuple-element.13), calls=%async_computation | async-start | bytes 524288 | tf_op jit(solution)/shard_map/all_to_all | solution.py:360
  13.4 2.7 %collective-permute-start.1 = (bf16[2,128,128]{2,1,0:T(8,128)(2,1)}, bf16[2,128,128]{2,1,0:T(8,128)(2,1)S(1)}, u32[]{:S(2)}, u32[]{:S(2)}) collective-permute-start(bf16[2,128,128]{2,1,0:T(8,128)(2,1)} %get-tuple-element.12.own), channel_id=1, source_target_pairs={{32,0},{64,32},{96,64},{0,96},{33,1},{65,33},{97,65},{1,97},{34,2}... | collective-permute-start | bytes 196616 | tf_op jit(solution)/shard_map/ppermute | solution.py:362
  16.0 0.0 collective-permute-start
  16.0 3.6 %weights.1 = (bf16[256,2304]{1,0:T(8,128)(2,1)}, bf16[2048,256]{1,0:T(8,128)(2,1)}, bf16[1536,256]{1,0:T(8,128)(2,1)}, bf16[128,256]{1,0:T(8,128)(2,1)}, bf16[1024,128]{1,0:T(8,128)(2,1)}) custom-call(bf16[2,128,128]{2,1,0:T(8,128)(2,1)} %get-tuple-element.12.own, bf16[9,28]{1,0:T(8,128)(2,1)} %bitcast.11, bf16[27,28,28]{2,1,0:T(8,128)(2,1)} %bitcast.8, ...), custom_call_target="tpu_custom_call" | custom-call | flops 100000000 | bytes 4000000 | tf_op jit(solution)/shard_map/weights/pallas_call | solution.py:365
  19.6 0.0 collective-permute-done.1.nxt
  19.6 0.0 copy-start.1
  19.6 1.3 %collective-permute-done.prev = bf16[2,128,128]{2,1,0:T(8,128)(2,1)S(1)} collective-permute-done((bf16[2,128,128]{2,1,0:T(8,128)(2,1)}, bf16[2,128,128]{2,1,0:T(8,128)(2,1)S(1)}, u32[]{:S(2)}, u32[]{:S(2)}) %collective-permute-start) | collective-permute-done | bytes 65568 | tf_op jit(solution)/shard_map/ppermute | solution.py:361
  20.9 0.0 copy-start.2
  20.9 3.4 %all-to-all-done.recv = bf16[128,8,128]{2,1,0:T(8,128)(2,1)S(1)} async-done(((bf16[128,8,128]{2,1,0:T(8,128)(2,1)}), bf16[128,8,128]{2,1,0:T(8,128)(2,1)S(1)}, u32[]{:S(2)}, u32[]{:S(2)}) %all-to-all-start) | async-done | bytes 262176 | tf_op jit(solution)/shard_map/all_to_all | solution.py:360
  24.3 0.0 copy-start
  24.3 0.0 copy-done.1
  24.3 0.0 copy-done.2
  24.3 0.7 %copy-done = bf16[128,8,128]{2,1,0:T(8,128)(2,1)} copy-done((bf16[128,8,128]{2,1,0:T(8,128)(2,1)}, bf16[128,8,128]{2,1,0:T(8,128)(2,1)S(1)}, u32[]{:S(2)}) %copy-start) | copy-done | bytes 262168
  25.0 20.8 %layers.1 = f32[1,3,2,128,128]{4,3,2,1,0:T(8,128)} custom-call(s32[1,8]{1,0:T(1,128)} %nb.3, s32[1,1]{1,0:T(1,128)} %bitcast.place.depth, bf16[2,128,128]{2,1,0:T(8,128)(2,1)} %copy-done.2, bf16[2,128,128]{2,1,0:T(8,128)(2,1)} %bitcast.7, bf16[2,128,128]{2,1,0:T(8,128)(2,1)} %copy-done.1, bf16[128,8,128]{2,1,0:T(8,128)(2,1)} %copy-done, ...), custom_call_target="tpu_custom_call" | custom-call | tf_op jit(solution)/shard_map/layers/pallas_call | solution.py:388
Async XLA Ops:
  1.9 22.4 %all-to-all-start = ((bf16[128,8,128]{2,1,0:T(8,128)(2,1)}), bf16[128,8,128]{2,1,0:T(8,128)(2,1)S(1)}, u32[]{:S(2)}, u32[]{:S(2)}) async-start(bf16[128,8,128]{2,1,0:T(8,128)(2,1)} %get-tuple-element.13), calls=%async_computation | async-start | bytes 524288 | tf_op jit(solution)/shard_map/all_to_all | solution.py:360
  13.4 6.2 %collective-permute-start.1 = (bf16[2,128,128]{2,1,0:T(8,128)(2,1)}, bf16[2,128,128]{2,1,0:T(8,128)(2,1)S(1)}, u32[]{:S(2)}, u32[]{:S(2)}) collective-permute-start(bf16[2,128,128]{2,1,0:T(8,128)(2,1)} %get-tuple-element.12.own), channel_id=1, source_target_pairs={{32,0},{64,32},{96,64},{0,96},{33,1},{65,33},{97,65},{1,97},{34,2}... | collective-permute-start | bytes 196616 | tf_op jit(solution)/shard_map/ppermute | solution.py:362
  16.0 4.8 %collective-permute-start = (bf16[2,128,128]{2,1,0:T(8,128)(2,1)}, bf16[2,128,128]{2,1,0:T(8,128)(2,1)S(1)}, u32[]{:S(2)}, u32[]{:S(2)}) collective-permute-start(bf16[2,128,128]{2,1,0:T(8,128)(2,1)} %get-tuple-element.12.own), channel_id=1, source_target_pairs={{0,32},{32,64},{64,96},{96,0},{1,33},{33,65},{65,97},{97,1},{2,34}... | collective-permute-start | bytes 196616 | tf_op jit(solution)/shard_map/ppermute | solution.py:361
  19.6 4.7 %copy-start.1 = (bf16[2,128,128]{2,1,0:T(8,128)(2,1)}, bf16[2,128,128]{2,1,0:T(8,128)(2,1)S(1)}, u32[]{:S(2)}) copy-start(bf16[2,128,128]{2,1,0:T(8,128)(2,1)S(1)} %collective-permute-done.1.nxt) | copy-start | bytes 196612
  20.9 3.4 %copy-start.2 = (bf16[2,128,128]{2,1,0:T(8,128)(2,1)}, bf16[2,128,128]{2,1,0:T(8,128)(2,1)S(1)}, u32[]{:S(2)}) copy-start(bf16[2,128,128]{2,1,0:T(8,128)(2,1)S(1)} %collective-permute-done.prev) | copy-start | bytes 196612
  24.3 0.7 %copy-start = (bf16[128,8,128]{2,1,0:T(8,128)(2,1)}, bf16[128,8,128]{2,1,0:T(8,128)(2,1)S(1)}, u32[]{:S(2)}) copy-start(bf16[128,8,128]{2,1,0:T(8,128)(2,1)S(1)} %all-to-all-done.recv) | copy-start | bytes 786436

commit v6 on v5

--- a/solution.py
+++ b/solution.py
@@ -226,15 +226,18 @@
         lines = [edge_taps[side, pl.ds(dy, 80), :].astype(BF16) for dy in range(3)]
         windows += [jnp.concatenate(lines[dy : dy + 2], axis=1) for dy in range(2)]
     edges = jnp.maximum(dot(jnp.concatenate(windows, axis=0), wf[...]), 0.0).astype(BF16)
-    for p in range(2):
-        pairs = []
-        for z in range(4):
-            for dy in range(2):
+    totals = [None, None]
+    for z in range(4):
+        for dy in range(2):
+            at = (z * 2 + dy) * 256
+            for p in range(2):
                 lanes = (2 * p + z) * 384
                 west = edges[dy * 80 : dy * 80 + 80, lanes + 128 : lanes + 384]
                 east = edges[160 + dy * 80 : 240 + dy * 80, lanes : lanes + 256]
-                pairs.append((jnp.concatenate([west, east], axis=0), ws[(z * 2 + dy) * 256 : (z * 2 + dy) * 256 + 256, :]))
-        value = jnp.maximum(add_dots(pairs), 0.0).astype(BF16)
+                term = dot(jnp.concatenate([west, east], axis=0), ws[at : at + 256, :])
+                totals[p] = term if totals[p] is None else totals[p] + term
+    for p in range(2):
+        value = jnp.maximum(totals[p], 0.0).astype(BF16)
         edge_mean[p, 0] = dot(value[0:80], pools[p][1])
         edge_mean[p, 1] = dot(value[80:160], pools[p][0])
 

time: 46 us -> 45.5 us (0.989)
  Pallas kernels: 26.2 us -> 25.7 us
where the time goes in v6:
time: 45.5 us; the launch traced here: 45.3 us
  Pallas kernels  25.7 us (56%)
  starting transfers between devices  14.2 us (31%)
  waiting for transfers between devices  4.68 us (10%)
  local copies, waits for them, and re-layouts  0.71 us (2%)
    pallas_call x1, Pallas kernels, on_device(): pl.pallas_call(main_kernel, out_shape=jax.ShapeDtypeStruct((1, 3, 2, 128,...  20.3 us
    all_to_all x1, starting transfers between devices, on_device(): recv = lax.all_to_all(slots, ('gz', 'xy'), 0, 0, tiled=True)  11.5 us
    pallas_call x1, Pallas kernels, on_device(): pl.pallas_call(weights_kernel, out_shape=[jax.ShapeDtypeStruct(s, BF16) f...  3.57 us
    all_to_all x1, waiting for transfers between devices, on_device(): recv = lax.all_to_all(slots, ('gz', 'xy'), 0, 0, tiled=True)  3.42 us
    ppermute x1, starting transfers between devices, on_device(): nxt = lax.ppermute(sent, 'gz', [((i + 1) % steps, i) for i in range(steps)])  2.67 us
    pallas_call x1, Pallas kernels, on_device(): pl.pallas_call(pack_kernel, out_shape=[jax.ShapeDtypeStruct((128, 8, 128)...  1.85 us
    ppermute x1, waiting for transfers between devices, on_device(): lax.ppermute(sent, 'gz', [(i, (i + 1) % steps) for i in range(steps)])  1.25 us
  transfers between devices with their start and end apart: 3, of which 2 were waited for; matrix products, arithmetic and copies ran while one was open for 0% of the time, Pallas kernels for 8%

profile of v6, /device:TPU:1, one launch (start us, length us, event | category | flops | bytes accessed | tf_op | source)
XLA Modules:
  0.0 45.3 jit_solution(11362848655942150302)
XLA Ops:
  0.0 1.8 %pack.1 = (bf16[128,8,128]{2,1,0:T(8,128)(2,1)}, bf16[2,128,128]{2,1,0:T(8,128)(2,1)}) custom-call(s32[1,8]{1,0:T(1,128)} %nb.3, s32[1,1]{1,0:T(1,128)} %bitcast.place.depth, bf16[2,128,128]{2,1,0:T(8,128)(2,1)} %bitcast.6), custom_call_target="tpu_custom_call" | custom-call | tf_op jit(solution)/shard_map/pack/pallas_call | solution.py:354
  1.8 11.5 %all-to-all-start = ((bf16[128,8,128]{2,1,0:T(8,128)(2,1)}), bf16[128,8,128]{2,1,0:T(8,128)(2,1)S(1)}, u32[]{:S(2)}, u32[]{:S(2)}) async-start(bf16[128,8,128]{2,1,0:T(8,128)(2,1)} %get-tuple-element.13), calls=%async_computation | async-start | bytes 524288 | tf_op jit(solution)/shard_map/all_to_all | solution.py:363
  13.3 2.7 %collective-permute-start.1 = (bf16[2,128,128]{2,1,0:T(8,128)(2,1)}, bf16[2,128,128]{2,1,0:T(8,128)(2,1)S(1)}, u32[]{:S(2)}, u32[]{:S(2)}) collective-permute-start(bf16[2,128,128]{2,1,0:T(8,128)(2,1)} %get-tuple-element.12.own), channel_id=1, source_target_pairs={{32,0},{64,32},{96,64},{0,96},{33,1},{65,33},{97,65},{1,97},{34,2}... | collective-permute-start | bytes 196616 | tf_op jit(solution)/shard_map/ppermute | solution.py:365
  16.0 0.0 collective-permute-start
  16.0 3.6 %weights.1 = (bf16[256,2304]{1,0:T(8,128)(2,1)}, bf16[2048,256]{1,0:T(8,128)(2,1)}, bf16[1536,256]{1,0:T(8,128)(2,1)}, bf16[128,256]{1,0:T(8,128)(2,1)}, bf16[1024,128]{1,0:T(8,128)(2,1)}) custom-call(bf16[2,128,128]{2,1,0:T(8,128)(2,1)} %get-tuple-element.12.own, bf16[9,28]{1,0:T(8,128)(2,1)} %bitcast.11, bf16[27,28,28]{2,1,0:T(8,128)(2,1)} %bitcast.8, ...), custom_call_target="tpu_custom_call" | custom-call | flops 100000000 | bytes 4000000 | tf_op jit(solution)/shard_map/weights/pallas_call | solution.py:368
  19.6 0.0 collective-permute-done.1.nxt
  19.6 0.0 copy-start.1
  19.6 1.3 %collective-permute-done.prev = bf16[2,128,128]{2,1,0:T(8,128)(2,1)S(1)} collective-permute-done((bf16[2,128,128]{2,1,0:T(8,128)(2,1)}, bf16[2,128,128]{2,1,0:T(8,128)(2,1)S(1)}, u32[]{:S(2)}, u32[]{:S(2)}) %collective-permute-start) | collective-permute-done | bytes 65568 | tf_op jit(solution)/shard_map/ppermute | solution.py:364
  20.9 0.0 copy-start.2
  20.9 3.4 %all-to-all-done.recv = bf16[128,8,128]{2,1,0:T(8,128)(2,1)S(1)} async-done(((bf16[128,8,128]{2,1,0:T(8,128)(2,1)}), bf16[128,8,128]{2,1,0:T(8,128)(2,1)S(1)}, u32[]{:S(2)}, u32[]{:S(2)}) %all-to-all-start) | async-done | bytes 262176 | tf_op jit(solution)/shard_map/all_to_all | solution.py:363
  24.3 0.0 copy-start
  24.3 0.0 copy-done.1
  24.3 0.0 copy-done.2
  24.3 0.7 %copy-done = bf16[128,8,128]{2,1,0:T(8,128)(2,1)} copy-done((bf16[128,8,128]{2,1,0:T(8,128)(2,1)}, bf16[128,8,128]{2,1,0:T(8,128)(2,1)S(1)}, u32[]{:S(2)}) %copy-start) | copy-done | bytes 262168
  25.0 20.3 %layers.1 = f32[1,3,2,128,128]{4,3,2,1,0:T(8,128)} custom-call(s32[1,8]{1,0:T(1,128)} %nb.3, s32[1,1]{1,0:T(1,128)} %bitcast.place.depth, bf16[2,128,128]{2,1,0:T(8,128)(2,1)} %copy-done.2, bf16[2,128,128]{2,1,0:T(8,128)(2,1)} %bitcast.7, bf16[2,128,128]{2,1,0:T(8,128)(2,1)} %copy-done.1, bf16[128,8,128]{2,1,0:T(8,128)(2,1)} %copy-done, ...), custom_call_target="tpu_custom_call" | custom-call | tf_op jit(solution)/shard_map/layers/pallas_call | solution.py:391
Async XLA Ops:
  1.8 22.4 %all-to-all-start = ((bf16[128,8,128]{2,1,0:T(8,128)(2,1)}), bf16[128,8,128]{2,1,0:T(8,128)(2,1)S(1)}, u32[]{:S(2)}, u32[]{:S(2)}) async-start(bf16[128,8,128]{2,1,0:T(8,128)(2,1)} %get-tuple-element.13), calls=%async_computation | async-start | bytes 524288 | tf_op jit(solution)/shard_map/all_to_all | solution.py:363
  13.3 6.2 %collective-permute-start.1 = (bf16[2,128,128]{2,1,0:T(8,128)(2,1)}, bf16[2,128,128]{2,1,0:T(8,128)(2,1)S(1)}, u32[]{:S(2)}, u32[]{:S(2)}) collective-permute-start(bf16[2,128,128]{2,1,0:T(8,128)(2,1)} %get-tuple-element.12.own), channel_id=1, source_target_pairs={{32,0},{64,32},{96,64},{0,96},{33,1},{65,33},{97,65},{1,97},{34,2}... | collective-permute-start | bytes 196616 | tf_op jit(solution)/shard_map/ppermute | solution.py:365
  16.0 4.8 %collective-permute-start = (bf16[2,128,128]{2,1,0:T(8,128)(2,1)}, bf16[2,128,128]{2,1,0:T(8,128)(2,1)S(1)}, u32[]{:S(2)}, u32[]{:S(2)}) collective-permute-start(bf16[2,128,128]{2,1,0:T(8,128)(2,1)} %get-tuple-element.12.own), channel_id=1, source_target_pairs={{0,32},{32,64},{64,96},{96,0},{1,33},{33,65},{65,97},{97,1},{2,34}... | collective-permute-start | bytes 196616 | tf_op jit(solution)/shard_map/ppermute | solution.py:364
  19.6 4.7 %copy-start.1 = (bf16[2,128,128]{2,1,0:T(8,128)(2,1)}, bf16[2,128,128]{2,1,0:T(8,128)(2,1)S(1)}, u32[]{:S(2)}) copy-start(bf16[2,128,128]{2,1,0:T(8,128)(2,1)S(1)} %collective-permute-done.1.nxt) | copy-start | bytes 196612
  20.9 3.4 %copy-start.2 = (bf16[2,128,128]{2,1,0:T(8,128)(2,1)}, bf16[2,128,128]{2,1,0:T(8,128)(2,1)S(1)}, u32[]{:S(2)}) copy-start(bf16[2,128,128]{2,1,0:T(8,128)(2,1)S(1)} %collective-permute-done.prev) | copy-start | bytes 196612
  24.3 0.7 %copy-start = (bf16[128,8,128]{2,1,0:T(8,128)(2,1)}, bf16[128,8,128]{2,1,0:T(8,128)(2,1)S(1)}, u32[]{:S(2)}) copy-start(bf16[128,8,128]{2,1,0:T(8,128)(2,1)S(1)} %all-to-all-done.recv) | copy-start | bytes 786436
